TPU v7x, 32 devices: a whole 2x2x4 slice. The times are simulated.
32 devices in a mesh: gx: 8 (over y, x, core), gy: 4 (over z).
Axes of the slice: x: 2, y: 2, z: 4, core: 2. Of those that a mesh axis runs over, the one named last changes fastest.
Arguments:
- hidden_states: bfloat16 [4, 256, 2048], P('gy', 'gx'), may hold values from -500 to 500
- norm_gain: float32 [2048], replicated, may hold values from 0.1 to 1.9
- norm_bias: float32 [2048], replicated, may hold values from -3 to 3
- query_weight: bfloat16 [2048, 2048], P('gy', 'gx'), may hold values from -0.125 to 0.125
- keyvalue_weight: bfloat16 [2048, 256], P('gy', 'gx'), may hold values from -0.125 to 0.125
- out_weight: bfloat16 [2048, 2048], P('gx', 'gy'), may hold values from -0.75 to 0.75
- key_cache: bfloat16 [4, 2304, 128], P('gy', 'gx'), may hold values from -400 to 400
- value_cache: bfloat16 [4, 2304, 128], P('gy', 'gx'), may hold values from -6 to 6
- cache_length: int32 [4], P('gy'), may hold values from 0 to 2048, as said below
Outputs:
- attention_out: bfloat16 [4, 256, 2048], P('gy', 'gx')
- new_key_cache: bfloat16 [4, 2304, 128], P('gy', 'gx')
- new_value_cache: bfloat16 [4, 2304, 128], P('gy', 'gx')
Inputs may be any that keep to these rules, and one draw needn't show every extreme that they name: Request r holds cache_length[r] earlier tokens; its new tokens take positions cache_length[r] to cache_length[r] + 255. Some request holds exactly 2048.
All inputs are finite; a program needn't handle non-finite values.
Results may differ from a plain program's by a relative error of at most 0.012.
The roundings to bfloat16 on the way count: a program that leaves them out, or rounds other values in their place, can miss the bound.
Values may be sent and summed in bfloat16 or wider, within the bound.
A program may use at most 192 MiB of HBM per device.

v0:
```python
import jax
import jax.numpy as jnp
from jax import lax
from jax.sharding import PartitionSpec as P

HEADS = 16


NEGATIVE = -1e30


def normalize(hidden_states, norm_gain, norm_bias):
    values = hidden_states.astype(jnp.float32)
    average = jnp.mean(values, axis=-1, keepdims=True)
    centred = values - average
    spread = jnp.mean(centred * centred, axis=-1, keepdims=True)
    return (centred * lax.rsqrt(spread + 1e-05) * norm_gain + norm_bias).astype(jnp.bfloat16)


def page_terms(query_rows, query_pos, key_rows, value_rows, page_size):
    row_count = query_rows.shape[0]
    head_dim = key_rows.shape[1]
    page_count = key_rows.shape[0] // page_size
    scores = lax.dot_general(
        query_rows, key_rows, (((1,), (1,)), ((), ())), preferred_element_type=jnp.float32
    )
    scores = (scores * head_dim ** (-0.5)).reshape(row_count, page_count, page_size)
    key_pos = jnp.arange(page_count * page_size, dtype=jnp.int32).reshape(page_count, page_size)
    allowed = key_pos[None, :, :] <= query_pos[:, None, None]
    maxima = jnp.max(jnp.where(allowed, scores, NEGATIVE), axis=2)
    weights = jnp.where(allowed, jnp.exp(scores - maxima[:, :, None]), 0.0)
    totals = jnp.sum(weights, axis=2)
    weighted = jnp.einsum(
        "rnp,npd->rnd",
        weights.astype(jnp.bfloat16),
        value_rows.reshape(page_count, page_size, head_dim),
        preferred_element_type=jnp.float32,
    )
    return (maxima, totals, weighted)


def reduce_pages(maxima, totals, weighted):
    largest = jnp.max(maxima, axis=1)
    factor = jnp.exp(maxima - largest[:, None])
    return (
        largest,
        jnp.sum(totals * factor, axis=1),
        jnp.sum(weighted * factor[:, :, None], axis=1),
    )


def join_pages(first, second):
    larger = jnp.maximum(first[0], second[0])
    second_factor = jnp.exp(second[0] - larger)
    return (larger, second[1] * second_factor, second[2] * second_factor[:, None])


def body(
    hidden_states,
    norm_gain,
    norm_bias,
    query_weight,
    keyvalue_weight,
    out_weight,
    key_cache,
    value_cache,
    cache_length,
):
    own_tokens = hidden_states.shape[1]
    groups = lax.axis_size("gx")
    column_index = lax.axis_index("gx")
    span_len = own_tokens * groups
    page_size = key_cache.shape[1]
    head_dim = key_cache.shape[2]
    head_count = HEADS
    head_width = head_count * head_dim
    normed = normalize(hidden_states[0], norm_gain, norm_bias)
    full_rows = lax.all_gather(normed, "gx", axis=0, tiled=True)
    pieces = (
        lax.all_gather(query_weight, "gy", axis=0, tiled=True),
        lax.all_gather(keyvalue_weight, "gy", axis=0, tiled=True),
    )
    query_part = jnp.dot(full_rows, pieces[0], preferred_element_type=jnp.float32)
    keyvalue_part = jnp.dot(full_rows, pieces[1], preferred_element_type=jnp.float32)
    query_local = query_part.astype(jnp.bfloat16)
    keyvalue_local = keyvalue_part.astype(jnp.bfloat16)
    queries, new_keyvalue = (
        lax.all_gather(query_local, "gx", axis=1, tiled=True),
        lax.all_gather(keyvalue_local, "gx", axis=1, tiled=True),
    )
    length = cache_length[0]
    page_base = column_index * page_size
    offsets = page_base + jnp.arange(page_size, dtype=jnp.int32) - length
    inside = (offsets >= 0) & (offsets < span_len)
    picked = jnp.take(new_keyvalue, jnp.clip(offsets, 0, span_len - 1), axis=0)
    key_page = jnp.where(inside[:, None], picked[:, :head_dim], key_cache[0])
    value_page = jnp.where(inside[:, None], picked[:, head_dim:], value_cache[0])
    own_rows = lax.dynamic_slice_in_dim(queries, column_index * own_tokens, own_tokens, 0)
    own_rows = own_rows.reshape(own_tokens * head_count, head_dim)
    own_pos = (
        length
        + column_index * own_tokens
        + jnp.arange(own_tokens * head_count, dtype=jnp.int32) // head_count
    )
    own_total = own_tokens * head_count
    empty = (
        jnp.full((own_total,), NEGATIVE, jnp.float32),
        jnp.zeros((own_total,), jnp.float32),
        jnp.zeros((own_total, head_dim), jnp.float32),
    )
    pieces = (
        lax.all_gather(key_page, "gx", axis=0, tiled=True),
        lax.all_gather(value_page, "gx", axis=0, tiled=True),
    )
    maxima, totals, weighted = page_terms(own_rows, own_pos, pieces[0], pieces[1], page_size)
    maxima, totals, weighted = join_pages(empty, reduce_pages(maxima, totals, weighted))
    own_out = (weighted / totals[:, None]).reshape(own_tokens, head_width).astype(jnp.bfloat16)
    attended = lax.all_to_all(own_out, "gx", split_axis=1, concat_axis=0, tiled=True)
    out_full = lax.all_gather(out_weight, "gy", axis=1, tiled=True)
    hidden_part = lax.psum_scatter(
        jnp.dot(attended, out_full, preferred_element_type=jnp.float32),
        "gx",
        scatter_dimension=0,
        tiled=True,
    )
    return (hidden_part.astype(jnp.bfloat16)[None], key_page[None], value_page[None])


def solution(mesh):
    return jax.shard_map(
        body,
        mesh=mesh,
        in_specs=(
            P("gy", "gx", None),
            P(),
            P(),
            P("gy", "gx"),
            P("gy", "gx"),
            P("gx", "gy"),
            P("gy", "gx", None),
            P("gy", "gx", None),
            P("gy"),
        ),
        out_specs=(P("gy", "gx", None), P("gy", "gx", None), P("gy", "gx", None)),
        check_vma=False,
    )
```

profile of v0, /device:TPU:0, one launch (start us, length us, event | category | flops | bytes accessed | tf_op | source)
XLA Modules:
  0.0 195.9 jit_solution(1756704536612807598)
XLA Ops:
  7.2 0.0 copy-start.4
  7.2 0.0 copy-start.3
  7.2 0.0 all-gather.7.cloned.1.call-start
  7.2 0.7 all-gather.7.cloned.1.call-update
  7.9 0.0 all-gather.5.cloned.1.call-start
  8.0 1.0 convert_reduce_fusion
  9.0 1.1 fusion.15
  10.1 1.7 fusion.18
  11.8 0.0 all-gather.5.cloned.1.call-update
  11.9 0.0 all-gather.9.cloned.1.call-start
  11.9 28.3 %all-gather.7.cloned.1.call-done = bf16[2048,256]{1,0:T(8,128)(2,1)} async-done(((bf16[512,256]{1,0:T(8,128)(2,1)}), bf16[2048,256]{1,0:T(8,128)(2,1)}) %all-gather.7.cloned.1.call-update) | async-done | bytes 1048592 | tf_op jit(solution)/shard_map/all_gather | solution.py:80
  40.3 25.5 %all-gather.5.cloned.1.call-done = bf16[256,2048]{1,0:T(8,128)(2,1)} async-done(((bf16[32,2048]{1,0:T(8,128)(2,1)}), bf16[256,2048]{1,0:T(8,128)(2,1)}) %all-gather.5.cloned.1.call-update) | async-done | bytes 1048592 | tf_op jit(solution)/shard_map/all_gather | solution.py:78
  65.7 2.6 %convolution_convert_fusion = bf16[256,256]{1,0:T(8,128)(2,1)} fusion(bf16[256,2048]{1,0:T(8,128)(2,1)} %all-gather.5.cloned.1.call-done, bf16[2048,256]{1,0:T(8,128)(2,1)} %all-gather.7.cloned.1.call-done), kind=kOutput, calls=%fused_computation.15 | convolution fusion | flops 268500992 | bytes 2228224 | tf_op jit(solution)/shard_map/dot_general | solution.py:83
  68.4 0.0 all-gather.9.cloned.1.call-update
  68.4 0.0 all-gather.11.cloned.1.call-start
  68.4 0.5 all-gather.11.cloned.1.call-update
  69.7 13.6 %all_gather.25 = bf16[2048,32]{0,1:T(8,128)(2,1)S(1)} all-gather(bf16[512,32]{0,1:T(8,128)(2,1)} %param.13), channel_id=1, replica_groups=mesh['gx'=8,'gy'=4] {'gy'}, dimensions={0}, use_global_device_ids=true | all-gather | bytes 163840 | tf_op jit(solution)/shard_map/all_gather | solution.py:81
  83.3 0.1 broadcast_in_dim_reshape.16
  83.4 1.6 convolution_convert_fusion.1
  85.1 9.2 %all_gather.26 = bf16[256,256]{0,1:T(8,128)(2,1)S(1)} all-gather(bf16[256,32]{0,1:T(8,128)(2,1)S(1)} %convolution_convert_fusion.1), channel_id=1, replica_groups=mesh['gx'=8,'gy'=4] {'gx'}, dimensions={1}, use_global_device_ids=true | all-gather | bytes 147456 | tf_op jit(solution)/shard_map/all_gather | solution.py:89
  94.3 0.1 copy.20
  94.4 2.0 %gather_fusion = bf16[288,256]{1,0:T(8,128)(2,1)S(1)} fusion(bf16[256,256]{1,0:T(8,128)(2,1)S(1)} %copy.20, s32[1024]{0:T(1024)S(1)} %pad_clamp_fusion), kind=kCustom, calls=%fused_computation | custom fusion | bytes 296064 | tf_op jit(solution)/shard_map/jit(_take)/gather | solution.py:95
  96.4 0.1 broadcast_select_fusion
  96.5 0.0 copy-done.4
  96.5 0.0 copy-done.3
  96.5 0.1 slice_select_fusion.1
  96.6 0.0 copy-start.1
  96.7 0.0 copy-start.2
  96.7 9.1 %all_gather.30 = bf16[2304,128]{1,0:T(8,128)(2,1)S(1)} all-gather(bf16[288,128]{1,0:T(8,128)(2,1)S(1)} %get-tuple-element.6), channel_id=1, replica_groups=mesh['gx'=8,'gy'=4] {'gx'}, dimensions={0}, use_global_device_ids=true | all-gather | bytes 663552 | tf_op jit(solution)/shard_map/all_gather | solution.py:112
  105.7 9.9 %all_gather.27 = bf16[2304,128]{1,0:T(8,128)(2,1)S(1)} all-gather(bf16[288,128]{1,0:T(8,128)(2,1)S(1)} %get-tuple-element.5), channel_id=1, replica_groups=mesh['gx'=8,'gy'=4] {'gx'}, dimensions={0}, use_global_device_ids=true | all-gather | bytes 663552 | tf_op jit(solution)/shard_map/all_gather | solution.py:113
  115.6 0.0 all-gather.9.cloned.1.call-done
  115.6 0.9 constant_dynamic-slice_fusion
  116.6 0.1 reshape.141
  116.6 3.1 %select_reduce_fusion = (f32[512]{0:T(512)S(1)}, f32[512,2304]{1,0:T(8,128)}) fusion(s32[2304]{0:T(1024)S(1)} %broadcast_in_dim_reshape.16, s32[512]{0:T(512)S(1)} %fusion.20, bf16[512,128]{1,0:T(8,128)(2,1)S(1)} %reshape.141, bf16[2304,128]{1,0:T(8,128)(2,1)S(1)} %all_gather.30), kind=kOutput, calls=%fused_computation.5 | convolution fusion | flops 306707968 | bytes 5452800 | tf_op jit(solution)/shard_map/dot_general | solution.py:24
  119.7 6.1 %copy.21 = f32[512,2304]{0,1:T(8,128)} copy(f32[512,2304]{1,0:T(8,128)} %get-tuple-element.10) | data formatting | bytes 9437184 | tf_op jit(solution)/shard_map/mul | solution.py:27
  125.8 0.0 copy-done.1
  125.8 0.0 copy-done.2
  125.8 2.7 %fusion = f32[512,8]{0,1:T(8,128)S(1)} fusion(f32[512,8,288]{0,2,1:T(8,128)} %bitcast.47, s32[512]{0:T(512)S(1)} %fusion.20, s32[8,288]{1,0:T(8,128)S(1)} %multiply_add_fusion), kind=kLoop, calls=%fused_computation.4 | loop fusion | flops 3534848 | bytes 4746240 | tf_op jit(solution)/shard_map/reduce_max | solution.py:30
  128.6 0.1 reduce_max.22
  128.6 0.0 copy-start
  128.6 3.0 %fusion.1 = f32[512,8]{0,1:T(8,128)S(1)} fusion(f32[512,8,288]{0,2,1:T(8,128)} %bitcast.48, f32[512,8]{0,1:T(8,128)S(1)} %fusion, s32[512]{0:T(512)S(1)} %fusion.20, s32[8,288]{1,0:T(8,128)S(1)} %multiply_add_fusion), kind=kLoop, calls=%fused_computation.6 | loop fusion | flops 4714496 | bytes 4762624 | tf_op jit(solution)/shard_map/reduce_sum | solution.py:32
  131.7 0.7 copy-done
  132.4 1.5 fusion.9
  133.9 0.1 copy.22
  134.0 0.1 reduce_sum.52
  134.1 0.1 reduce_sum.55
  134.2 0.1 div.30
  134.3 0.1 div.31
  134.4 0.1 mul.73
  134.5 0.1 mul.74
  134.6 0.1 divide_convert_fusion
  134.7 0.7 copy.23
  135.4 3.4 %all-to-all-start = ((bf16[32,8,256]{2,0,1:T(8,128)(2,1)}), bf16[32,8,256]{2,0,1:T(8,128)(2,1)S(1)}, u32[]{:S(2)}, u32[]{:S(2)}) async-start(bf16[32,8,256]{2,0,1:T(8,128)(2,1)} %copy.23), calls=%async_computation | async-start | bytes 262144 | tf_op jit(solution)/shard_map/all_to_all | solution.py:118
  138.8 0.0 reduce-scatter.2.cloned.1.call-start
  138.8 0.0 all-gather.11.cloned.1.call-done
  138.8 5.4 %all-to-all-done = bf16[32,8,256]{2,0,1:T(8,128)(2,1)S(1)} async-done(((bf16[32,8,256]{2,0,1:T(8,128)(2,1)}), bf16[32,8,256]{2,0,1:T(8,128)(2,1)S(1)}, u32[]{:S(2)}, u32[]{:S(2)}) %all-to-all-start) | async-done | bytes 131104 | tf_op jit(solution)/shard_map/all_to_all | solution.py:118
  144.2 3.0 %fusion.30 = f32[256,2048]{1,0:T(8,128)} fusion(bf16[256,256]{1,0:T(8,128)(2,1)S(1)} %bitcast.51, bf16[256,2048]{1,0:T(8,128)(2,1)} %all-gather.11.cloned.1.call-done), kind=kOutput, calls=%fused_computation.58 | convolution fusion | flops 268435456 | bytes 3276800 | tf_op jit(solution)/shard_map/dot_general | solution.py:121
  147.2 0.0 reduce-scatter.2.cloned.1.call-update
  147.3 40.5 %reduce-scatter.2.cloned.1.call-done = f32[32,2048]{1,0:T(8,128)} async-done(((f32[256,2048]{1,0:T(8,128)}), f32[32,2048]{1,0:T(8,128)}) %reduce-scatter.2.cloned.1.call-update) | async-done | bytes 262160 | tf_op jit(solution)/shard_map/reduce_scatter | solution.py:120
  187.8 1.6 convert_bitcast_fusion.1
  (10 shorter events, 0.1 us)
Async XLA Ops:
  7.2 89.3 %copy-start.4 = (bf16[1,288,128]{2,1,0:T(8,128)(2,1)S(1)}, bf16[1,288,128]{2,1,0:T(8,128)(2,1)}, u32[]{:S(2)}) copy-start(bf16[1,288,128]{2,1,0:T(8,128)(2,1)} %param.15) | copy-start | bytes 221188
  7.2 89.3 %copy-start.3 = (bf16[1,288,128]{2,1,0:T(8,128)(2,1)S(1)}, bf16[1,288,128]{2,1,0:T(8,128)(2,1)}, u32[]{:S(2)}) copy-start(bf16[1,288,128]{2,1,0:T(8,128)(2,1)} %param.16) | copy-start | bytes 221188
  7.2 33.1 %all-gather.7.cloned.1.call-start = ((), (), s32[]{:S(2)}) async-start(), calls=%async_computation.3 | async-start | bytes 1310720 | tf_op jit(solution)/shard_map/all_gather | solution.py:80
  7.9 57.8 %all-gather.5.cloned.1.call-start = ((), (), s32[]{:S(2)}) async-start(), calls=%async_computation.2 | async-start | bytes 1179648 | tf_op jit(solution)/shard_map/all_gather | solution.py:78
  11.9 103.8 %all-gather.9.cloned.1.call-start = ((), (), s32[]{:S(2)}) async-start(), calls=%async_computation.4 | async-start | bytes 1179648 | tf_op jit(solution)/shard_map/all_gather | solution.py:88
  68.4 70.4 %all-gather.11.cloned.1.call-start = ((), (), s32[]{:S(2)}) async-start(), calls=%async_computation.5 | async-start | bytes 1310720 | tf_op jit(solution)/shard_map/all_gather | solution.py:119
  96.6 29.2 %copy-start.1 = (bf16[288,128]{1,0:T(8,128)(2,1)}, bf16[288,128]{1,0:T(8,128)(2,1)S(1)}, u32[]{:S(2)}) copy-start(bf16[288,128]{1,0:T(8,128)(2,1)S(1)} %get-tuple-element.5) | copy-start | bytes 221188
  96.7 29.2 %copy-start.2 = (bf16[288,128]{1,0:T(8,128)(2,1)}, bf16[288,128]{1,0:T(8,128)(2,1)S(1)}, u32[]{:S(2)}) copy-start(bf16[288,128]{1,0:T(8,128)(2,1)S(1)} %get-tuple-element.6) | copy-start | bytes 221188
  128.6 3.8 %copy-start = (f32[512,2304]{0,1:T(8,128)S(1)}, f32[512,2304]{0,1:T(8,128)}, u32[]{:S(2)}) copy-start(f32[512,2304]{0,1:T(8,128)} %copy.21) | copy-start | bytes 14155780
  135.4 8.8 %all-to-all-start = ((bf16[32,8,256]{2,0,1:T(8,128)(2,1)}), bf16[32,8,256]{2,0,1:T(8,128)(2,1)S(1)}, u32[]{:S(2)}, u32[]{:S(2)}) async-start(bf16[32,8,256]{2,0,1:T(8,128)(2,1)} %copy.23), calls=%async_computation | async-start | bytes 262144 | tf_op jit(solution)/shard_map/all_to_all | solution.py:118
  138.8 49.0 %reduce-scatter.2.cloned.1.call-start = ((), (), s32[]{:S(2)}) async-start(), calls=%async_computation.6 | async-start | bytes 2359296 | tf_op jit(solution)/shard_map/reduce_scatter | solution.py:120
Sparse Core Ops, SparseCore 0:
  9.6 30.6 all-gather.6
  42.7 22.9 all-gather.4
  68.5 23.7 all-gather.8
  93.7 27.9 all-gather.10
  147.4 40.3 reduce-scatter.1
where the time goes:
time: 196 us
  waiting for transfers between devices  101 us (52%)
  blocking collectives  41.8 us (21%)
  between operations  14.7 us (8%)
  matrix products  11.8 us (6%)
  other arithmetic  11.6 us (6%)
  local copies, waits for them, and re-layouts  11.4 us (6%)
  starting transfers between devices  3.57 us (2%)
    reduce_scatter x1, waiting for transfers between devices, body(): lax.psum_scatter(jnp.dot(attended, out_full, preferred_element_type=jnp.f...  40.5 us
    all_gather x1, waiting for transfers between devices, body(): lax.all_gather(query_weight, 'gy', axis=0, tiled=True)  28.3 us
    all_gather x1, waiting for transfers between devices, body(): full_rows = lax.all_gather(normed, 'gx', axis=0, tiled=True)  25.5 us
    all_gather x1, blocking collectives, body(): lax.all_gather(keyvalue_weight, 'gy', axis=0, tiled=True)  13.6 us
    all_gather x1, blocking collectives, body(): lax.all_gather(value_page, 'gx', axis=0, tiled=True)  9.92 us
    all_gather x1, blocking collectives, body(): lax.all_gather(keyvalue_local, 'gx', axis=1, tiled=True)  9.23 us
    all_gather x1, blocking collectives, body(): lax.all_gather(key_page, 'gx', axis=0, tiled=True)  9.06 us
    mul x1, local copies, waits for them, and re-layouts, page_terms(): scores * head_dim ** (-0.5)  6.13 us
  transfers between devices with their start and end apart: 6, of which 4 were waited for; matrix products, arithmetic and copies ran while one was open for 14% of the time, Pallas kernels for 0%

commit v1 on v0

--- a/solution.py
+++ b/solution.py
@@ -1,6 +1,11 @@
+import functools
+import math
+
 import jax
 import jax.numpy as jnp
 from jax import lax
+from jax.experimental import pallas as pl
+from jax.experimental.pallas import tpu as pltpu
 from jax.sharding import PartitionSpec as P
 
 HEADS = 16
@@ -126,9 +131,493 @@
     return (hidden_part.astype(jnp.bfloat16)[None], key_page[None], value_page[None])
 
 
+MESH = pl.DeviceIdType.MESH
+CHIPS = 4
+FLIPS = 3
+
+
+def fused_kernel(
+    planes,
+    hidden_ref,
+    gain_ref,
+    bias_ref,
+    wq_ref,
+    wkv_ref,
+    wo_ref,
+    key_ref,
+    value_ref,
+    length_ref,
+    out_ref,
+    new_key_ref,
+    new_value_ref,
+    normed,
+    wq_all,
+    wkv_all,
+    wo_all,
+    keys,
+    values,
+    new_kv,
+    query_rows,
+    attended,
+    partial,
+    sibling_out,
+    sibling_in,
+    chip_out,
+    chip_in,
+    own_sum,
+    load_sem,
+    z_send,
+    z_recv,
+    rows_send,
+    rows_recv,
+    kv_send,
+    kv_recv,
+    sib_send,
+    sib_recv,
+    chip_send,
+    chip_recv,
+):
+    me = lax.axis_index("gx")
+    z = lax.axis_index("gy")
+    core = me % 2
+    chip = me // 2
+    cx = chip % 2
+    cy = chip // 2
+    sibling = chip * 2 + 1 - core
+    other_chips = (cy * 2 + 1 - cx, (1 - cy) * 2 + cx, (1 - cy) * 2 + 1 - cx)
+    peers = [other * 2 + core for other in other_chips]
+    far = [other * 2 + 1 - core for other in other_chips]
+    everyone = [sibling] + peers + far
+    has_up = z < planes - 1
+    has_down = z > 0
+
+    barrier = pltpu.get_barrier_semaphore()
+    for peer in everyone:
+        pl.semaphore_signal(barrier, inc=1, device_id={"gx": peer}, device_id_type=MESH)
+
+    @pl.when(has_up)
+    def _():
+        pl.semaphore_signal(barrier, inc=1, device_id={"gy": z + 1}, device_id_type=MESH)
+
+    @pl.when(has_down)
+    def _():
+        pl.semaphore_signal(barrier, inc=1, device_id={"gy": z - 1}, device_id_type=MESH)
+
+    loads = [
+        pltpu.make_async_copy(wq_ref, wq_all.at[z], load_sem.at[0]),
+        pltpu.make_async_copy(wo_ref, wo_all.at[z], load_sem.at[1]),
+        pltpu.make_async_copy(key_ref, keys.at[me], load_sem.at[2]),
+        pltpu.make_async_copy(value_ref, values.at[me], load_sem.at[3]),
+    ]
+    for load in loads:
+        load.start()
+
+    rows = hidden_ref[...].astype(jnp.float32)
+    average = jnp.mean(rows, axis=-1, keepdims=True)
+    centred = rows - average
+    spread = jnp.mean(centred * centred, axis=-1, keepdims=True)
+    normed[me] = (
+        centred * lax.rsqrt(spread + 1e-05) * gain_ref[...] + bias_ref[...]
+    ).astype(jnp.bfloat16)
+    wkv_all[z] = wkv_ref[...].astype(jnp.float32).T.astype(jnp.bfloat16)
+
+    neighbours = has_up.astype(jnp.int32) + has_down.astype(jnp.int32)
+    pl.semaphore_wait(barrier, len(everyone) + neighbours)
+
+    def z_copy(kind, buffer, step, direction):
+        shard = z - direction * step
+        return pltpu.make_async_remote_copy(
+            src_ref=buffer.at[shard],
+            dst_ref=buffer.at[shard],
+            send_sem=z_send.at[kind, step, (direction + 1) // 2],
+            recv_sem=z_recv.at[kind, shard],
+            device_id={"gy": z + direction},
+            device_id_type=MESH,
+        )
+
+    def z_cond(step, direction):
+        if direction > 0:
+            return has_up & (z - step >= 0)
+        return has_down & (z + step < planes)
+
+    def z_start(kind, buffer, step):
+        for direction in (1, -1):
+
+            @pl.when(z_cond(step, direction))
+            def _(direction=direction):
+                z_copy(kind, buffer, step, direction).start()
+
+    def z_wait_send(kind, buffer, step):
+        for direction in (1, -1):
+
+            @pl.when(z_cond(step, direction))
+            def _(direction=direction):
+                z_copy(kind, buffer, step, direction).wait_send()
+
+    def z_wait_recv(kind, buffer, step):
+        for direction in (1, -1):
+            shard = z - direction * (step + 1)
+
+            @pl.when((shard >= 0) & (shard < planes))
+            def _(shard=shard):
+                pltpu.make_async_copy(
+                    buffer.at[shard], buffer.at[shard], z_recv.at[kind, shard]
+                ).wait()
+
+    gathered = (normed, keys, values)
+
+    def row_copy(kind, block, target, slot):
+        return pltpu.make_async_remote_copy(
+            src_ref=gathered[kind].at[block],
+            dst_ref=gathered[kind].at[block],
+            send_sem=rows_send.at[kind, slot],
+            recv_sem=rows_recv.at[kind, block],
+            device_id={"gx": target},
+            device_id_type=MESH,
+        )
+
+    def rows_start(kind):
+        for slot, target in enumerate(peers + [sibling]):
+            row_copy(kind, me, target, slot).start()
+
+    def rows_wait(kind, block):
+        pltpu.make_async_copy(
+            gathered[kind].at[block], gathered[kind].at[block], rows_recv.at[kind, block]
+        ).wait()
+
+    def rows_forward(kind):
+        for flip in range(FLIPS):
+            rows_wait(kind, peers[flip])
+            row_copy(kind, peers[flip], sibling, 4 + flip).start()
+
+    def rows_finish(kind):
+        for block in [sibling] + far:
+            rows_wait(kind, block)
+
+    z_start(0, wkv_all, 0)
+    loads[0].wait()
+    z_start(1, wq_all, 0)
+    rows_start(0)
+    loads[2].wait()
+    rows_start(1)
+    loads[3].wait()
+    rows_start(2)
+    loads[1].wait()
+
+    z_wait_recv(0, wkv_all, 0)
+    z_start(0, wkv_all, 1)
+    z_wait_recv(0, wkv_all, 1)
+    z_start(0, wkv_all, 2)
+    rows_forward(0)
+    z_wait_recv(1, wq_all, 0)
+    z_start(1, wq_all, 1)
+    rows_finish(0)
+    z_wait_recv(0, wkv_all, 2)
+
+    tokens = normed[...].reshape(-1, normed.shape[2])
+    token_count = tokens.shape[0]
+    depth = wq_all.shape[1]
+    kv_width = wkv_all.shape[1]
+    kv_part = jnp.zeros((kv_width, token_count), jnp.float32)
+    for part in range(planes):
+        kv_part += lax.dot_general(
+            wkv_all[part],
+            tokens[:, part * depth : (part + 1) * depth],
+            (((1,), (1,)), ((), ())),
+            preferred_element_type=jnp.float32,
+        )
+    new_kv[me] = kv_part.astype(jnp.bfloat16)
+
+    def kv_copy(block, target, slot):
+        return pltpu.make_async_remote_copy(
+            src_ref=new_kv.at[block],
+            dst_ref=new_kv.at[block],
+            send_sem=kv_send.at[slot],
+            recv_sem=kv_recv.at[block],
+            device_id={"gx": target},
+            device_id_type=MESH,
+        )
+
+    for slot, target in enumerate(everyone):
+        kv_copy(me, target, slot).start()
+
+    rows_forward(1)
+    rows_forward(2)
+    z_wait_recv(1, wq_all, 1)
+    z_start(1, wq_all, 2)
+    z_start(2, wo_all, 0)
+
+    for block in everyone:
+        pltpu.make_async_copy(new_kv.at[block], new_kv.at[block], kv_recv.at[block]).wait()
+
+    length = length_ref[0]
+    page = key_ref.shape[0]
+    head_dim = key_ref.shape[1]
+    kv_cols = new_kv[...].reshape(2 * head_dim, token_count)
+    offsets = (
+        lax.broadcasted_iota(jnp.int32, (page, token_count), 0) + me * page - length
+    )
+    chosen = offsets == lax.broadcasted_iota(jnp.int32, (page, token_count), 1)
+    picked = lax.dot_general(
+        jnp.where(chosen, 1.0, 0.0).astype(jnp.bfloat16),
+        kv_cols,
+        (((1,), (1,)), ((), ())),
+        preferred_element_type=jnp.float32,
+    )
+    row_offset = lax.broadcasted_iota(jnp.int32, (page, head_dim), 0) + me * page - length
+    inside = (row_offset >= 0) & (row_offset < token_count)
+    new_key_ref[...] = jnp.where(
+        inside, picked[:, :head_dim], keys[me].astype(jnp.float32)
+    ).astype(jnp.bfloat16)
+    new_value_ref[...] = jnp.where(
+        inside, picked[:, head_dim:], values[me].astype(jnp.float32)
+    ).astype(jnp.bfloat16)
+
+    rows_finish(1)
+    rows_finish(2)
+    z_wait_recv(1, wq_all, 2)
+
+    heads = wq_all.shape[2] // head_dim
+    query = jnp.zeros((token_count, heads * head_dim), jnp.float32)
+    for part in range(planes):
+        query += jnp.dot(
+            normed[:, :, part * depth : (part + 1) * depth].reshape(token_count, depth),
+            wq_all[part],
+            preferred_element_type=jnp.float32,
+        )
+    query = query.astype(jnp.bfloat16)
+    for head in range(heads):
+        query_rows[head * token_count : (head + 1) * token_count, :] = query[
+            :, head * head_dim : (head + 1) * head_dim
+        ]
+
+    cached = keys.shape[0] * page - token_count
+    block_rows = 128
+    scale = head_dim ** (-0.5) * math.log2(math.e)
+
+    def attend(start):
+        first = pl.multiple_of(start * block_rows, block_rows)
+        q = query_rows[pl.ds(first, block_rows), :]
+        old_keys = keys[...].reshape(-1, head_dim)[:cached]
+        old_values = values[...].reshape(-1, head_dim)[:cached]
+        fresh = new_kv[...].reshape(2 * head_dim, token_count)
+        old_pos = lax.broadcasted_iota(jnp.int32, (block_rows, cached), 1)
+        old = lax.dot_general(
+            q, old_keys, (((1,), (1,)), ((), ())), preferred_element_type=jnp.float32
+        )
+        old = jnp.where(old_pos < length, old * scale, NEGATIVE)
+        row = lax.broadcasted_iota(jnp.int32, (block_rows, token_count), 0) + first % token_count
+        col = lax.broadcasted_iota(jnp.int32, (block_rows, token_count), 1)
+        new = jnp.dot(q, fresh[:head_dim], preferred_element_type=jnp.float32)
+        new = jnp.where(col <= row, new * scale, NEGATIVE)
+        top = jnp.maximum(
+            jnp.max(old, axis=1, keepdims=True), jnp.max(new, axis=1, keepdims=True)
+        )
+        old = jnp.exp2(old - top)
+        new = jnp.exp2(new - top)
+        total = jnp.sum(old, axis=1, keepdims=True) + jnp.sum(new, axis=1, keepdims=True)
+        summed = jnp.dot(
+            old.astype(jnp.bfloat16), old_values, preferred_element_type=jnp.float32
+        ) + lax.dot_general(
+            new.astype(jnp.bfloat16),
+            fresh[head_dim:],
+            (((1,), (1,)), ((), ())),
+            preferred_element_type=jnp.float32,
+        )
+        attended[pl.ds(first, block_rows), :] = (summed / total).astype(jnp.bfloat16)
+
+    pl.loop(0, heads * token_count // block_rows)(attend)
+
+    own_rows = hidden_ref.shape[0]
+    width = wo_all.shape[2]
+    result_rows = jnp.concatenate(
+        [attended[head * token_count : (head + 1) * token_count, :] for head in range(heads)],
+        axis=1,
+    )
+
+    def sib_copy(n):
+        return pltpu.make_async_remote_copy(
+            src_ref=sibling_out.at[n],
+            dst_ref=sibling_in.at[n],
+            send_sem=sib_send.at[n],
+            recv_sem=sib_recv.at[n],
+            device_id={"gx": sibling},
+            device_id_type=MESH,
+        )
+
+    def chip_copy(n, flip):
+        return pltpu.make_async_remote_copy(
+            src_ref=chip_out.at[n, flip],
+            dst_ref=chip_in.at[n, flip],
+            send_sem=chip_send.at[n, flip],
+            recv_sem=chip_recv.at[n, flip],
+            device_id={"gx": peers[flip]},
+            device_id_type=MESH,
+        )
+
+    def project(n, shard):
+        partial[n] = jnp.dot(
+            result_rows, wo_all[shard], preferred_element_type=jnp.float32
+        ).reshape(2 * CHIPS, own_rows, width)
+        for k in range(CHIPS):
+            sibling_out[n, k] = partial[n, 2 * k + 1 - core].astype(jnp.bfloat16)
+        sib_copy(n).start()
+
+    def spread_sums(n):
+        sib_copy(n).wait_recv()
+        for flip in range(FLIPS):
+            other = other_chips[flip]
+            chip_out[n, flip] = (
+                partial[n, 2 * other + core] + sibling_in[n, other].astype(jnp.float32)
+            ).astype(jnp.bfloat16)
+            chip_copy(n, flip).start()
+        own_sum[n] = partial[n, me] + sibling_in[n, chip].astype(jnp.float32)
+
+    low = z < planes // 2
+    order = [z, jnp.where(low, z + 1, z - 1)]
+    order.append(jnp.where(low, (z + planes - 1) % planes, (z + 1) % planes))
+    order[2] = jnp.where((z == 0) | (z == planes - 1), jnp.where(low, 2, planes - 3), order[2])
+    order.append(jnp.where(low, planes - 1, 0))
+
+    project(0, order[0])
+    z_wait_recv(2, wo_all, 0)
+    z_start(2, wo_all, 1)
+    project(1, order[1])
+    spread_sums(0)
+    z_wait_recv(2, wo_all, 1)
+    z_start(2, wo_all, 2)
+    project(2, order[2])
+    spread_sums(1)
+    z_wait_recv(2, wo_all, 2)
+    project(3, order[3])
+    spread_sums(2)
+    spread_sums(3)
+    for n in range(planes):
+        total = own_sum[n]
+        for flip in range(FLIPS):
+            chip_copy(n, flip).wait_recv()
+            total += chip_in[n, flip].astype(jnp.float32)
+        column = pl.multiple_of(order[n] * width, width)
+        out_ref[:, pl.ds(column, width)] = total.astype(jnp.bfloat16)
+
+    for kind, buffer in enumerate((wkv_all, wq_all, wo_all)):
+        for step in range(planes - 1):
+            z_wait_send(kind, buffer, step)
+    for kind in range(3):
+        for slot, target in enumerate(peers + [sibling]):
+            row_copy(kind, me, target, slot).wait_send()
+        for flip in range(FLIPS):
+            row_copy(kind, peers[flip], sibling, 4 + flip).wait_send()
+    for slot, target in enumerate(everyone):
+        kv_copy(me, target, slot).wait_send()
+    for n in range(planes):
+        sib_copy(n).wait_send()
+        for flip in range(FLIPS):
+            chip_copy(n, flip).wait_send()
+
+
+def fused(
+    groups,
+    planes,
+    hidden_states,
+    norm_gain,
+    norm_bias,
+    query_weight,
+    keyvalue_weight,
+    out_weight,
+    key_cache,
+    value_cache,
+    cache_length,
+):
+    own_rows, model = hidden_states.shape[1:]
+    page, head_dim = key_cache.shape[1:]
+    span = own_rows * groups
+    depth, columns = query_weight.shape
+    kv_width = keyvalue_weight.shape[1]
+    out_rows, width = out_weight.shape
+    heads = columns // head_dim
+    bf16, f32 = jnp.bfloat16, jnp.float32
+    vmem = pl.BlockSpec(memory_space=pltpu.VMEM)
+    anywhere = pl.BlockSpec(memory_space=pl.ANY)
+    dma = pltpu.SemaphoreType.DMA
+    out, new_key, new_value = pl.pallas_call(
+        functools.partial(fused_kernel, planes),
+        out_shape=(
+            jax.ShapeDtypeStruct((own_rows, model), bf16),
+            jax.ShapeDtypeStruct((page, head_dim), bf16),
+            jax.ShapeDtypeStruct((page, head_dim), bf16),
+        ),
+        in_specs=[
+            vmem,
+            vmem,
+            vmem,
+            anywhere,
+            vmem,
+            anywhere,
+            anywhere,
+            anywhere,
+            pl.BlockSpec(memory_space=pltpu.SMEM),
+        ],
+        out_specs=(vmem, vmem, vmem),
+        scratch_shapes=[
+            pltpu.VMEM((groups, own_rows, model), bf16),
+            pltpu.VMEM((planes, depth, columns), bf16),
+            pltpu.VMEM((planes, kv_width, depth), bf16),
+            pltpu.VMEM((planes, out_rows, width), bf16),
+            pltpu.VMEM((groups, page, head_dim), bf16),
+            pltpu.VMEM((groups, page, head_dim), bf16),
+            pltpu.VMEM((groups, kv_width, span), bf16),
+            pltpu.VMEM((heads * span, head_dim), bf16),
+            pltpu.VMEM((heads * span, head_dim), bf16),
+            pltpu.VMEM((planes, 2 * CHIPS, own_rows, width), f32),
+            pltpu.VMEM((planes, CHIPS, own_rows, width), bf16),
+            pltpu.VMEM((planes, CHIPS, own_rows, width), bf16),
+            pltpu.VMEM((planes, FLIPS, own_rows, width), bf16),
+            pltpu.VMEM((planes, FLIPS, own_rows, width), bf16),
+            pltpu.VMEM((planes, own_rows, width), f32),
+            dma((4,)),
+            dma((3, planes - 1, 2)),
+            dma((3, planes)),
+            dma((3, 4 + FLIPS)),
+            dma((3, groups)),
+            dma((groups - 1,)),
+            dma((groups,)),
+            dma((planes,)),
+            dma((planes,)),
+            dma((planes, FLIPS)),
+            dma((planes, FLIPS)),
+        ],
+        compiler_params=pltpu.CompilerParams(
+            collective_id=0, has_side_effects=True, vmem_limit_bytes=48 * 1024 * 1024
+        ),
+        cost_estimate=pl.CostEstimate(
+            flops=10**9, bytes_accessed=2 * 10**6, transcendentals=10**6
+        ),
+        name="attention_layer",
+    )(
+        hidden_states[0],
+        norm_gain[None],
+        norm_bias[None],
+        query_weight,
+        keyvalue_weight,
+        out_weight,
+        key_cache[0],
+        value_cache[0],
+        cache_length,
+    )
+    return out[None], new_key[None], new_value[None]
+
+
+def device_program(mesh, *args):
+    groups, planes = mesh.shape["gx"], mesh.shape["gy"]
+    if groups == 2 * CHIPS and planes == 4:
+        return fused(groups, planes, *args)
+    return body(*args)
+
+
 def solution(mesh):
     return jax.shard_map(
-        body,
+        functools.partial(device_program, mesh),
         mesh=mesh,
         in_specs=(
             P("gy", "gx", None),

time: 196 us -> 58.3 us (0.30)
  waiting for transfers between devices: 101 us -> 0 us
  Pallas kernels: 0 us -> 50.1 us
  blocking collectives: 41.8 us -> 0 us
  between operations: 14.7 us -> 1.38 us
  matrix products: 11.8 us -> 0 us
  other arithmetic: 11.6 us -> 0 us
  local copies, waits for them, and re-layouts: 11.4 us -> 6.49 us
  starting transfers between devices: 3.57 us -> 0 us
    all_gather x4 -> x0, waiting for transfers between devices: 53.8 us -> none  [the longest x1 28.3 us: body(): lax.all_gather(query_weight, 'gy', axis=0, tiled=True)]
    pallas_call x0 -> x1, Pallas kernels: none -> 50.1 us  [fused(): pl.pallas_call(functools.partial(fused_kernel, planes), out_shape=(jax.Sh...]
    all_gather x4 -> x0, blocking collectives: 41.8 us -> none  [the longest x1 13.6 us: body(): lax.all_gather(keyvalue_weight, 'gy', axis=0, tiled=True)]
    reduce_scatter x1 -> x0, waiting for transfers between devices: 40.5 us -> none  [body(): lax.psum_scatter(jnp.dot(attended, out_full, preferred_element_type=jnp.f...]
    dot_general x5 -> x0, matrix products: 11.8 us -> none  [the longest x1 3.06 us: page_terms(): lax.dot_general(query_rows, key_rows, (((1,), (1,)), ((), ())), preferred...]
    mul x3 -> x0, local copies, waits for them, and re-layouts: 6.32 us -> none  [the longest x1 6.13 us: page_terms(): scores * head_dim ** (-0.5)]
    unnamed x10 -> x18, local copies, waits for them, and re-layouts: 0.71 us -> 6.49 us
    all_to_all x1 -> x0, waiting for transfers between devices: 5.39 us -> none  [body(): lax.all_to_all(own_out, 'gx', split_axis=1, concat_axis=0, tiled=True)]
  transfers between devices with their start and end apart: 6 -> 0, of which waited for: 4 -> 0; matrix products, arithmetic and copies ran while one was open for 14% -> 0% of each run, Pallas kernels for 0% -> 0%
where the time goes in v1:
time: 58.3 us; the launch traced here: 58 us
  Pallas kernels  50.1 us (86%)
  local copies, waits for them, and re-layouts  6.49 us (11%)
  between operations  1.38 us (2%)
    pallas_call x1, Pallas kernels, fused(): pl.pallas_call(functools.partial(fused_kernel, planes), out_shape=(jax.Sh...  50.1 us
    unnamed x18, local copies, waits for them, and re-layouts  6.49 us

profile of v1, /device:TPU:0, one launch (start us, length us, event | category | flops | bytes accessed | tf_op | source)
XLA Modules:
  0.0 58.0 jit_solution(16943241935050384331)
XLA Ops:
  0.6 0.0 copy-start.2
  1.3 0.0 copy-start.5
  1.3 0.0 copy-start.6
  1.3 0.9 %copy.12.wkv_ref = bf16[512,32]{1,0:T(8,128)(2,1)S(1)} copy(bf16[512,32]{0,1:T(8,128)(2,1)} %param.13) | data formatting | bytes 65536 | tf_op args[4]
  2.2 0.0 copy-done.2
  2.2 0.0 copy-done.5
  2.3 0.0 copy-done.6
  2.3 0.0 copy-start
  2.3 0.9 %copy-done = bf16[512,256]{1,0:T(8,128)(2,1)S(1)} copy-done((bf16[512,256]{1,0:T(8,128)(2,1)S(1)}, bf16[512,256]{1,0:T(8,128)(2,1)}, u32[]{:S(2)}) %copy-start) | copy-done | bytes 262168
  3.2 0.0 copy-start.1
  3.2 0.9 %copy-done.1 = bf16[256,512]{1,0:T(8,128)(2,1)S(1)} copy-done((bf16[256,512]{1,0:T(8,128)(2,1)S(1)}, bf16[256,512]{1,0:T(8,128)(2,1)}, u32[]{:S(2)}) %copy-start.1) | copy-done | bytes 262168
  4.2 0.0 copy-start.3
  4.2 0.9 %copy-done.3 = bf16[1,288,128]{2,1,0:T(8,128)(2,1)S(1)} copy-done((bf16[1,288,128]{2,1,0:T(8,128)(2,1)S(1)}, bf16[1,288,128]{2,1,0:T(8,128)(2,1)}, u32[]{:S(2)}) %copy-start.3) | copy-done | bytes 73752
  5.1 0.0 copy-start.4
  5.1 0.9 %copy-done.4 = bf16[1,288,128]{2,1,0:T(8,128)(2,1)S(1)} copy-done((bf16[1,288,128]{2,1,0:T(8,128)(2,1)S(1)}, bf16[1,288,128]{2,1,0:T(8,128)(2,1)}, u32[]{:S(2)}) %copy-start.4) | copy-done | bytes 73752
  5.9 50.1 %attention_layer.1 = (bf16[32,2048]{1,0:T(8,128)(2,1)S(1)}, bf16[288,128]{1,0:T(8,128)(2,1)S(1)}, bf16[288,128]{1,0:T(8,128)(2,1)S(1)}) custom-call(bf16[32,2048]{1,0:T(8,128)(2,1)S(1)} %bitcast.11, f32[1,2048]{1,0:T(1,128)S(1)} %bitcast.14, f32[1,2048]{1,0:T(1,128)S(1)} %bitcast.15, bf16[512,256]{1,0:T(8,128)(2,1)S(1)} %copy-done, ...), custom_call_target="tpu_custom_call" | custom-call | flops 1000000000 | bytes 2000000 | tf_op jit(solution)/shard_map/attention_layer/pallas_call | solution.py:543
  56.1 0.7 %copy.17 = bf16[1,32,2048]{2,1,0:T(8,128)(2,1)} copy(bf16[1,32,2048]{2,1,0:T(8,128)(2,1)S(1)} %bitcast.8) | data formatting | bytes 262144
  56.7 0.6 %copy.18 = bf16[1,288,128]{2,1,0:T(8,128)(2,1)} copy(bf16[1,288,128]{2,1,0:T(8,128)(2,1)S(1)} %bitcast.10) | data formatting | bytes 147456
  57.4 0.6 %copy.19 = bf16[1,288,128]{2,1,0:T(8,128)(2,1)} copy(bf16[1,288,128]{2,1,0:T(8,128)(2,1)S(1)} %bitcast.9) | data formatting | bytes 147456
Async XLA Ops:
  0.6 1.6 %copy-start.2 = (bf16[1,32,2048]{2,1,0:T(8,128)(2,1)S(1)}, bf16[1,32,2048]{2,1,0:T(8,128)(2,1)}, u32[]{:S(2)}) copy-start(bf16[1,32,2048]{2,1,0:T(8,128)(2,1)} %param.9) | copy-start | bytes 393220
  1.3 0.9 %copy-start.5 = (f32[2048]{0:T(1024)S(1)}, f32[2048]{0:T(1024)}, u32[]{:S(2)}) copy-start(f32[2048]{0:T(1024)} %param.10) | copy-start | bytes 24580
  1.3 0.9 %copy-start.6 = (f32[2048]{0:T(1024)S(1)}, f32[2048]{0:T(1024)}, u32[]{:S(2)}) copy-start(f32[2048]{0:T(1024)} %param.11) | copy-start | bytes 24580
  2.3 1.0 %copy-start = (bf16[512,256]{1,0:T(8,128)(2,1)S(1)}, bf16[512,256]{1,0:T(8,128)(2,1)}, u32[]{:S(2)}) copy-start(bf16[512,256]{1,0:T(8,128)(2,1)} %wq_ref.1) | copy-start | bytes 786436
  3.2 0.9 %copy-start.1 = (bf16[256,512]{1,0:T(8,128)(2,1)S(1)}, bf16[256,512]{1,0:T(8,128)(2,1)}, u32[]{:S(2)}) copy-start(bf16[256,512]{1,0:T(8,128)(2,1)} %wo_ref.1) | copy-start | bytes 786436
  4.2 0.9 %copy-start.3 = (bf16[1,288,128]{2,1,0:T(8,128)(2,1)S(1)}, bf16[1,288,128]{2,1,0:T(8,128)(2,1)}, u32[]{:S(2)}) copy-start(bf16[1,288,128]{2,1,0:T(8,128)(2,1)} %param.15) | copy-start | bytes 221188
  5.1 0.9 %copy-start.4 = (bf16[1,288,128]{2,1,0:T(8,128)(2,1)S(1)}, bf16[1,288,128]{2,1,0:T(8,128)(2,1)}, u32[]{:S(2)}) copy-start(bf16[1,288,128]{2,1,0:T(8,128)(2,1)} %param.16) | copy-start | bytes 221188

commit v2 on v1

--- a/solution.py
+++ b/solution.py
@@ -150,6 +150,9 @@
     out_ref,
     new_key_ref,
     new_value_ref,
+    hidden_in,
+    gain_in,
+    bias_in,
     normed,
     wq_all,
     wkv_all,
@@ -203,31 +206,36 @@
     def _():
         pl.semaphore_signal(barrier, inc=1, device_id={"gy": z - 1}, device_id_type=MESH)
 
+    half_depth = wq_all.shape[2]
+    half_width = wo_all.shape[3]
+    half_rows = [wq_ref.at[pl.ds(half * half_depth, half_depth)] for half in range(2)]
+    half_cols = [wo_ref.at[:, pl.ds(half * half_width, half_width)] for half in range(2)]
+    sources = [wkv_ref] + half_rows + half_cols
+    buffers = [wkv_all, wq_all.at[0], wq_all.at[1], wo_all.at[0], wo_all.at[1]]
     loads = [
-        pltpu.make_async_copy(wq_ref, wq_all.at[z], load_sem.at[0]),
-        pltpu.make_async_copy(wo_ref, wo_all.at[z], load_sem.at[1]),
-        pltpu.make_async_copy(key_ref, keys.at[me], load_sem.at[2]),
-        pltpu.make_async_copy(value_ref, values.at[me], load_sem.at[3]),
+        pltpu.make_async_copy(source, target, load_sem.at[slot])
+        for slot, (source, target) in enumerate(
+            [
+                (hidden_ref, hidden_in),
+                (gain_ref, gain_in),
+                (bias_ref, bias_in),
+                (key_ref, keys.at[me]),
+                (value_ref, values.at[me]),
+            ]
+            + [(source, buffer.at[z]) for source, buffer in zip(sources, buffers)]
+        )
     ]
     for load in loads:
         load.start()
 
-    rows = hidden_ref[...].astype(jnp.float32)
-    average = jnp.mean(rows, axis=-1, keepdims=True)
-    centred = rows - average
-    spread = jnp.mean(centred * centred, axis=-1, keepdims=True)
-    normed[me] = (
-        centred * lax.rsqrt(spread + 1e-05) * gain_ref[...] + bias_ref[...]
-    ).astype(jnp.bfloat16)
-    wkv_all[z] = wkv_ref[...].astype(jnp.float32).T.astype(jnp.bfloat16)
-
     neighbours = has_up.astype(jnp.int32) + has_down.astype(jnp.int32)
     pl.semaphore_wait(barrier, len(everyone) + neighbours)
 
-    def z_copy(kind, buffer, step, direction):
+    def z_copy(kind, step, direction):
         shard = z - direction * step
+        buffer = buffers[kind]
         return pltpu.make_async_remote_copy(
-            src_ref=buffer.at[shard],
+            src_ref=sources[kind] if step == 0 else buffer.at[shard],
             dst_ref=buffer.at[shard],
             send_sem=z_send.at[kind, step, (direction + 1) // 2],
             recv_sem=z_recv.at[kind, shard],
@@ -240,29 +248,43 @@
             return has_up & (z - step >= 0)
         return has_down & (z + step < planes)
 
-    def z_start(kind, buffer, step):
+    def z_arrived(kind, shard):
+        buffer = buffers[kind]
+        pltpu.make_async_copy(buffer.at[shard], buffer.at[shard], z_recv.at[kind, shard]).wait()
+
+    def z_forward(kind, step):
         for direction in (1, -1):
 
             @pl.when(z_cond(step, direction))
             def _(direction=direction):
-                z_copy(kind, buffer, step, direction).start()
-
-    def z_wait_send(kind, buffer, step):
+                if step > 0:
+                    z_arrived(kind, z - direction * step)
+                z_copy(kind, step, direction).start()
+
+    def z_wait_send(kind, step):
         for direction in (1, -1):
 
             @pl.when(z_cond(step, direction))
             def _(direction=direction):
-                z_copy(kind, buffer, step, direction).wait_send()
-
-    def z_wait_recv(kind, buffer, step):
+                z_copy(kind, step, direction).wait_send()
+
+    def z_last(kind, step):
+        @pl.when((z == planes - 1) & (z - 1 - step >= 0))
+        def _():
+            z_arrived(kind, z - 1 - step)
+
+        @pl.when((z == 0) & (z + 1 + step < planes))
+        def _():
+            z_arrived(kind, z + 1 + step)
+
+    def out_start(step):
         for direction in (1, -1):
-            shard = z - direction * (step + 1)
-
-            @pl.when((shard >= 0) & (shard < planes))
-            def _(shard=shard):
-                pltpu.make_async_copy(
-                    buffer.at[shard], buffer.at[shard], z_recv.at[kind, shard]
-                ).wait()
+            last = z if direction > 0 else planes - 1 - z
+
+            @pl.when(z_cond(0, direction) & (last == step))
+            def _(direction=direction):
+                z_copy(3, 0, direction).start()
+                z_copy(4, 0, direction).start()
 
     gathered = (normed, keys, values)
 
@@ -294,29 +316,38 @@
         for block in [sibling] + far:
             rows_wait(kind, block)
 
-    z_start(0, wkv_all, 0)
-    loads[0].wait()
-    z_start(1, wq_all, 0)
+    for kind in range(3):
+        z_forward(kind, 0)
+    out_start(0)
+
+    for slot in range(3):
+        loads[slot].wait()
+    rows = hidden_in[...].astype(jnp.float32)
+    average = jnp.mean(rows, axis=-1, keepdims=True)
+    centred = rows - average
+    spread = jnp.mean(centred * centred, axis=-1, keepdims=True)
+    normed[me] = (
+        centred * lax.rsqrt(spread + 1e-05) * gain_in[...] + bias_in[...]
+    ).astype(jnp.bfloat16)
     rows_start(0)
-    loads[2].wait()
-    rows_start(1)
-    loads[3].wait()
-    rows_start(2)
-    loads[1].wait()
-
-    z_wait_recv(0, wkv_all, 0)
-    z_start(0, wkv_all, 1)
-    z_wait_recv(0, wkv_all, 1)
-    z_start(0, wkv_all, 2)
+    for kind in (1, 2):
+        loads[kind + 2].wait()
+        rows_start(kind)
+
+    z_forward(0, 1)
+    z_forward(0, 2)
+    z_forward(1, 1)
     rows_forward(0)
-    z_wait_recv(1, wq_all, 0)
-    z_start(1, wq_all, 1)
+    z_forward(2, 1)
+    out_start(1)
     rows_finish(0)
-    z_wait_recv(0, wkv_all, 2)
+    loads[5].wait()
+    for step in range(planes - 1):
+        z_last(0, step)
 
     tokens = normed[...].reshape(-1, normed.shape[2])
     token_count = tokens.shape[0]
-    depth = wq_all.shape[1]
+    depth = 2 * half_depth
     kv_width = wkv_all.shape[1]
     kv_part = jnp.zeros((kv_width, token_count), jnp.float32)
     for part in range(planes):
@@ -342,10 +373,10 @@
         kv_copy(me, target, slot).start()
 
     rows_forward(1)
+    z_forward(1, 2)
     rows_forward(2)
-    z_wait_recv(1, wq_all, 1)
-    z_start(1, wq_all, 2)
-    z_start(2, wo_all, 0)
+    z_forward(2, 2)
+    out_start(2)
 
     for block in everyone:
         pltpu.make_async_copy(new_kv.at[block], new_kv.at[block], kv_recv.at[block]).wait()
@@ -375,14 +406,19 @@
 
     rows_finish(1)
     rows_finish(2)
-    z_wait_recv(1, wq_all, 2)
-
-    heads = wq_all.shape[2] // head_dim
+    for half in range(2):
+        loads[6 + half].wait()
+        for step in range(planes - 1):
+            z_last(1 + half, step)
+
+    heads = wq_all.shape[3] // head_dim
     query = jnp.zeros((token_count, heads * head_dim), jnp.float32)
-    for part in range(planes):
+    for part in range(2 * planes):
         query += jnp.dot(
-            normed[:, :, part * depth : (part + 1) * depth].reshape(token_count, depth),
-            wq_all[part],
+            normed[:, :, part * half_depth : (part + 1) * half_depth].reshape(
+                token_count, half_depth
+            ),
+            wq_all[part % 2, part // 2],
             preferred_element_type=jnp.float32,
         )
     query = query.astype(jnp.bfloat16)
@@ -426,10 +462,13 @@
         )
         attended[pl.ds(first, block_rows), :] = (summed / total).astype(jnp.bfloat16)
 
-    pl.loop(0, heads * token_count // block_rows)(attend)
+    blocks = heads * token_count // block_rows
+    pl.loop(0, blocks // 2)(attend)
+    z_forward(3, 1)
+    z_forward(4, 1)
+    pl.loop(blocks // 2, blocks)(attend)
 
     own_rows = hidden_ref.shape[0]
-    width = wo_all.shape[2]
     result_rows = jnp.concatenate(
         [attended[head * token_count : (head + 1) * token_count, :] for head in range(heads)],
         axis=1,
@@ -455,10 +494,10 @@
             device_id_type=MESH,
         )
 
-    def project(n, shard):
+    def project(n):
         partial[n] = jnp.dot(
-            result_rows, wo_all[shard], preferred_element_type=jnp.float32
-        ).reshape(2 * CHIPS, own_rows, width)
+            result_rows, wo_all[n % 2, order[n // 2]], preferred_element_type=jnp.float32
+        ).reshape(2 * CHIPS, own_rows, half_width)
         for k in range(CHIPS):
             sibling_out[n, k] = partial[n, 2 * k + 1 - core].astype(jnp.bfloat16)
         sib_copy(n).start()
@@ -479,30 +518,30 @@
     order[2] = jnp.where((z == 0) | (z == planes - 1), jnp.where(low, 2, planes - 3), order[2])
     order.append(jnp.where(low, planes - 1, 0))
 
-    project(0, order[0])
-    z_wait_recv(2, wo_all, 0)
-    z_start(2, wo_all, 1)
-    project(1, order[1])
-    spread_sums(0)
-    z_wait_recv(2, wo_all, 1)
-    z_start(2, wo_all, 2)
-    project(2, order[2])
-    spread_sums(1)
-    z_wait_recv(2, wo_all, 2)
-    project(3, order[3])
-    spread_sums(2)
-    spread_sums(3)
-    for n in range(planes):
+    slices = 2 * planes
+    for n in range(slices):
+        step = n // 2 - 1
+        if n < 2:
+            loads[8 + n].wait()
+        else:
+            z_last(3 + n % 2, step)
+        if n >= 2 and step + 1 == 1:
+            z_forward(3 + n % 2, 2)
+        project(n)
+        if n > 0:
+            spread_sums(n - 1)
+    spread_sums(slices - 1)
+    for n in range(slices):
         total = own_sum[n]
         for flip in range(FLIPS):
             chip_copy(n, flip).wait_recv()
             total += chip_in[n, flip].astype(jnp.float32)
-        column = pl.multiple_of(order[n] * width, width)
-        out_ref[:, pl.ds(column, width)] = total.astype(jnp.bfloat16)
-
-    for kind, buffer in enumerate((wkv_all, wq_all, wo_all)):
+        column = pl.multiple_of(order[n // 2] * 2 * half_width + n % 2 * half_width, half_width)
+        out_ref[:, pl.ds(column, half_width)] = total.astype(jnp.bfloat16)
+
+    for kind in range(5):
         for step in range(planes - 1):
-            z_wait_send(kind, buffer, step)
+            z_wait_send(kind, step)
     for kind in range(3):
         for slot, target in enumerate(peers + [sibling]):
             row_copy(kind, me, target, slot).wait_send()
@@ -510,7 +549,7 @@
             row_copy(kind, peers[flip], sibling, 4 + flip).wait_send()
     for slot, target in enumerate(everyone):
         kv_copy(me, target, slot).wait_send()
-    for n in range(planes):
+    for n in range(slices):
         sib_copy(n).wait_send()
         for flip in range(FLIPS):
             chip_copy(n, flip).wait_send()
@@ -538,7 +577,7 @@
     heads = columns // head_dim
     bf16, f32 = jnp.bfloat16, jnp.float32
     vmem = pl.BlockSpec(memory_space=pltpu.VMEM)
-    anywhere = pl.BlockSpec(memory_space=pl.ANY)
+    hbm = pl.BlockSpec(memory_space=pltpu.HBM)
     dma = pltpu.SemaphoreType.DMA
     out, new_key, new_value = pl.pallas_call(
         functools.partial(fused_kernel, planes),
@@ -547,48 +586,41 @@
             jax.ShapeDtypeStruct((page, head_dim), bf16),
             jax.ShapeDtypeStruct((page, head_dim), bf16),
         ),
-        in_specs=[
-            vmem,
-            vmem,
-            vmem,
-            anywhere,
-            vmem,
-            anywhere,
-            anywhere,
-            anywhere,
-            pl.BlockSpec(memory_space=pltpu.SMEM),
-        ],
+        in_specs=[hbm] * 8 + [pl.BlockSpec(memory_space=pltpu.SMEM)],
         out_specs=(vmem, vmem, vmem),
         scratch_shapes=[
+            pltpu.VMEM((own_rows, model), bf16),
+            pltpu.VMEM((1, model), f32),
+            pltpu.VMEM((1, model), f32),
             pltpu.VMEM((groups, own_rows, model), bf16),
-            pltpu.VMEM((planes, depth, columns), bf16),
+            pltpu.VMEM((2, planes, depth // 2, columns), bf16),
             pltpu.VMEM((planes, kv_width, depth), bf16),
-            pltpu.VMEM((planes, out_rows, width), bf16),
+            pltpu.VMEM((2, planes, out_rows, width // 2), bf16),
             pltpu.VMEM((groups, page, head_dim), bf16),
             pltpu.VMEM((groups, page, head_dim), bf16),
             pltpu.VMEM((groups, kv_width, span), bf16),
             pltpu.VMEM((heads * span, head_dim), bf16),
             pltpu.VMEM((heads * span, head_dim), bf16),
-            pltpu.VMEM((planes, 2 * CHIPS, own_rows, width), f32),
-            pltpu.VMEM((planes, CHIPS, own_rows, width), bf16),
-            pltpu.VMEM((planes, CHIPS, own_rows, width), bf16),
-            pltpu.VMEM((planes, FLIPS, own_rows, width), bf16),
-            pltpu.VMEM((planes, FLIPS, own_rows, width), bf16),
-            pltpu.VMEM((planes, own_rows, width), f32),
-            dma((4,)),
-            dma((3, planes - 1, 2)),
-            dma((3, planes)),
+            pltpu.VMEM((2 * planes, 2 * CHIPS, own_rows, width // 2), f32),
+            pltpu.VMEM((2 * planes, CHIPS, own_rows, width // 2), bf16),
+            pltpu.VMEM((2 * planes, CHIPS, own_rows, width // 2), bf16),
+            pltpu.VMEM((2 * planes, FLIPS, own_rows, width // 2), bf16),
+            pltpu.VMEM((2 * planes, FLIPS, own_rows, width // 2), bf16),
+            pltpu.VMEM((2 * planes, own_rows, width // 2), f32),
+            dma((10,)),
+            dma((5, planes - 1, 2)),
+            dma((5, planes)),
             dma((3, 4 + FLIPS)),
             dma((3, groups)),
             dma((groups - 1,)),
             dma((groups,)),
-            dma((planes,)),
-            dma((planes,)),
-            dma((planes, FLIPS)),
-            dma((planes, FLIPS)),
+            dma((2 * planes,)),
+            dma((2 * planes,)),
+            dma((2 * planes, FLIPS)),
+            dma((2 * planes, FLIPS)),
         ],
         compiler_params=pltpu.CompilerParams(
-            collective_id=0, has_side_effects=True, vmem_limit_bytes=48 * 1024 * 1024
+            collective_id=0, has_side_effects=True, vmem_limit_bytes=64 * 1024 * 1024
         ),
         cost_estimate=pl.CostEstimate(
             flops=10**9, bytes_accessed=2 * 10**6, transcendentals=10**6
@@ -599,7 +631,7 @@
         norm_gain[None],
         norm_bias[None],
         query_weight,
-        keyvalue_weight,
+        keyvalue_weight.T,
         out_weight,
         key_cache[0],
         value_cache[0],

time: 58.3 us -> 54.8 us (0.940)
  local copies, waits for them, and re-layouts: 6.49 us -> 3.15 us
    unnamed x18 -> x7, local copies, waits for them, and re-layouts: 6.49 us -> 3.15 us
where the time goes in v2:
time: 54.8 us; the launch traced here: 54.6 us
  Pallas kernels  50.2 us (92%)
  local copies, waits for them, and re-layouts  3.15 us (6%)
  between operations  1.3 us (2%)
    pallas_call x1, Pallas kernels, fused(): pl.pallas_call(functools.partial(fused_kernel, planes), out_shape=(jax.Sh...  50.2 us
    unnamed x7, local copies, waits for them, and re-layouts  3.15 us

profile of v2, /device:TPU:0, one launch (start us, length us, event | category | flops | bytes accessed | tf_op | source)
XLA Modules:
  0.0 54.6 jit_solution(1156013950809457448)
XLA Ops:
  1.3 50.2 %attention_layer.1 = (bf16[32,2048]{1,0:T(8,128)(2,1)}, bf16[288,128]{1,0:T(8,128)(2,1)}, bf16[288,128]{1,0:T(8,128)(2,1)}) custom-call(bf16[32,2048]{1,0:T(8,128)(2,1)} %bitcast.12, f32[1,2048]{1,0:T(1,128)} %bitcast.16, f32[1,2048]{1,0:T(1,128)} %bitcast.17, bf16[512,256]{1,0:T(8,128)(2,1)} %wq_ref.1, bf16[32,512]{1,0:T(8,128)(2,1)} %bitcast.15, ...), custom_call_target="tpu_custom_call" | custom-call | flops 1000000000 | bytes 2000000 | tf_op jit(solution)/shard_map/attention_layer/pallas_call | solution.py:582
  51.4 0.0 copy-start.1
  51.5 1.6 %copy.16 = bf16[1,32,2048]{2,1,0:T(8,128)(2,1)} copy(bf16[1,32,2048]{2,1,0:T(8,128)(2,1)} %bitcast.9) | data formatting | bytes 262144
  53.1 0.0 copy-done.1
  53.1 0.0 copy-start
  53.1 0.6 %copy.17 = bf16[1,288,128]{2,1,0:T(8,128)(2,1)} copy(bf16[1,288,128]{2,1,0:T(8,128)(2,1)S(1)} %bitcast.11) | data formatting | bytes 147456
  53.7 0.3 copy-done
  54.0 0.6 %copy.18 = bf16[1,288,128]{2,1,0:T(8,128)(2,1)} copy(bf16[1,288,128]{2,1,0:T(8,128)(2,1)S(1)} %bitcast.10) | data formatting | bytes 147456
Async XLA Ops:
  51.4 1.6 %copy-start.1 = (bf16[288,128]{1,0:T(8,128)(2,1)S(1)}, bf16[288,128]{1,0:T(8,128)(2,1)}, u32[]{:S(2)}) copy-start(bf16[288,128]{1,0:T(8,128)(2,1)} %get-tuple-element.7) | copy-start | bytes 221188
  53.1 0.9 %copy-start = (bf16[288,128]{1,0:T(8,128)(2,1)S(1)}, bf16[288,128]{1,0:T(8,128)(2,1)}, u32[]{:S(2)}) copy-start(bf16[288,128]{1,0:T(8,128)(2,1)} %get-tuple-element.8) | copy-start | bytes 221188

commit v3 on v2

--- a/solution.py
+++ b/solution.py
@@ -156,7 +156,7 @@
     normed,
     wq_all,
     wkv_all,
-    wo_all,
+    wo_own,
     keys,
     values,
     new_kv,
@@ -168,6 +168,7 @@
     chip_out,
     chip_in,
     own_sum,
+    pieces,
     load_sem,
     z_send,
     z_recv,
@@ -179,6 +180,8 @@
     sib_recv,
     chip_send,
     chip_recv,
+    home_send,
+    home_recv,
 ):
     me = lax.axis_index("gx")
     z = lax.axis_index("gy")
@@ -198,20 +201,14 @@
     for peer in everyone:
         pl.semaphore_signal(barrier, inc=1, device_id={"gx": peer}, device_id_type=MESH)
 
-    @pl.when(has_up)
-    def _():
-        pl.semaphore_signal(barrier, inc=1, device_id={"gy": z + 1}, device_id_type=MESH)
-
-    @pl.when(has_down)
-    def _():
-        pl.semaphore_signal(barrier, inc=1, device_id={"gy": z - 1}, device_id_type=MESH)
+    other_planes = [lax.rem(z + k, planes) for k in range(1, planes)]
+    for plane in other_planes:
+        pl.semaphore_signal(barrier, inc=1, device_id={"gy": plane}, device_id_type=MESH)
 
     half_depth = wq_all.shape[2]
-    half_width = wo_all.shape[3]
     half_rows = [wq_ref.at[pl.ds(half * half_depth, half_depth)] for half in range(2)]
-    half_cols = [wo_ref.at[:, pl.ds(half * half_width, half_width)] for half in range(2)]
-    sources = [wkv_ref] + half_rows + half_cols
-    buffers = [wkv_all, wq_all.at[0], wq_all.at[1], wo_all.at[0], wo_all.at[1]]
+    sources = [wkv_ref] + half_rows
+    buffers = [wkv_all, wq_all.at[0], wq_all.at[1], attended.at[0], attended.at[1]]
     loads = [
         pltpu.make_async_copy(source, target, load_sem.at[slot])
         for slot, (source, target) in enumerate(
@@ -223,19 +220,19 @@
                 (value_ref, values.at[me]),
             ]
             + [(source, buffer.at[z]) for source, buffer in zip(sources, buffers)]
+            + [(wo_ref, wo_own)]
         )
     ]
     for load in loads:
         load.start()
 
-    neighbours = has_up.astype(jnp.int32) + has_down.astype(jnp.int32)
-    pl.semaphore_wait(barrier, len(everyone) + neighbours)
-
-    def z_copy(kind, step, direction):
+    pl.semaphore_wait(barrier, len(everyone) + planes - 1)
+
+    def z_copy(kind, step, direction, own=False):
         shard = z - direction * step
         buffer = buffers[kind]
         return pltpu.make_async_remote_copy(
-            src_ref=sources[kind] if step == 0 else buffer.at[shard],
+            src_ref=sources[kind] if own and kind < len(sources) else buffer.at[shard],
             dst_ref=buffer.at[shard],
             send_sem=z_send.at[kind, step, (direction + 1) // 2],
             recv_sem=z_recv.at[kind, shard],
@@ -259,14 +256,14 @@
             def _(direction=direction):
                 if step > 0:
                     z_arrived(kind, z - direction * step)
-                z_copy(kind, step, direction).start()
+                z_copy(kind, step, direction, step == 0).start()
 
     def z_wait_send(kind, step):
         for direction in (1, -1):
 
             @pl.when(z_cond(step, direction))
             def _(direction=direction):
-                z_copy(kind, step, direction).wait_send()
+                z_copy(kind, step, direction, step == 0).wait_send()
 
     def z_last(kind, step):
         @pl.when((z == planes - 1) & (z - 1 - step >= 0))
@@ -277,14 +274,16 @@
         def _():
             z_arrived(kind, z + 1 + step)
 
-    def out_start(step):
-        for direction in (1, -1):
-            last = z if direction > 0 else planes - 1 - z
-
-            @pl.when(z_cond(0, direction) & (last == step))
-            def _(direction=direction):
-                z_copy(3, 0, direction).start()
-                z_copy(4, 0, direction).start()
+    def z_take(kind, shard):
+        z_arrived(kind, shard)
+
+        @pl.when((shard < z) & has_up)
+        def _():
+            z_copy(kind, z - shard, 1).start()
+
+        @pl.when((shard > z) & has_down)
+        def _():
+            z_copy(kind, shard - z, -1).start()
 
     gathered = (normed, keys, values)
 
@@ -318,7 +317,6 @@
 
     for kind in range(3):
         z_forward(kind, 0)
-    out_start(0)
 
     for slot in range(3):
         loads[slot].wait()
@@ -339,7 +337,6 @@
     z_forward(1, 1)
     rows_forward(0)
     z_forward(2, 1)
-    out_start(1)
     rows_finish(0)
     loads[5].wait()
     for step in range(planes - 1):
@@ -376,7 +373,6 @@
     z_forward(1, 2)
     rows_forward(2)
     z_forward(2, 2)
-    out_start(2)
 
     for block in everyone:
         pltpu.make_async_copy(new_kv.at[block], new_kv.at[block], kv_recv.at[block]).wait()
@@ -422,18 +418,23 @@
             preferred_element_type=jnp.float32,
         )
     query = query.astype(jnp.bfloat16)
-    for head in range(heads):
-        query_rows[head * token_count : (head + 1) * token_count, :] = query[
-            :, head * head_dim : (head + 1) * head_dim
-        ]
+    own_rows = hidden_ref.shape[0]
+    half_own = own_rows // 2
+    half_rows = token_count // 2
+    query = query.reshape(2 * CHIPS, own_rows, heads * head_dim)
+    for half in range(2):
+        rows_of_half = query[:, half * half_own : (half + 1) * half_own].reshape(half_rows, -1)
+        for head in range(heads):
+            query_rows[half * heads + head] = rows_of_half[
+                :, head * head_dim : (head + 1) * head_dim
+            ]
 
     cached = keys.shape[0] * page - token_count
-    block_rows = 128
+    block_rows = half_rows
     scale = head_dim ** (-0.5) * math.log2(math.e)
 
-    def attend(start):
-        first = pl.multiple_of(start * block_rows, block_rows)
-        q = query_rows[pl.ds(first, block_rows), :]
+    def attend(half, head):
+        q = query_rows[half * heads + head]
         old_keys = keys[...].reshape(-1, head_dim)[:cached]
         old_values = values[...].reshape(-1, head_dim)[:cached]
         fresh = new_kv[...].reshape(2 * head_dim, token_count)
@@ -442,7 +443,8 @@
             q, old_keys, (((1,), (1,)), ((), ())), preferred_element_type=jnp.float32
         )
         old = jnp.where(old_pos < length, old * scale, NEGATIVE)
-        row = lax.broadcasted_iota(jnp.int32, (block_rows, token_count), 0) + first % token_count
+        row = lax.broadcasted_iota(jnp.int32, (block_rows, token_count), 0)
+        row = row // half_own * own_rows + half * half_own + row % half_own
         col = lax.broadcasted_iota(jnp.int32, (block_rows, token_count), 1)
         new = jnp.dot(q, fresh[:head_dim], preferred_element_type=jnp.float32)
         new = jnp.where(col <= row, new * scale, NEGATIVE)
@@ -460,19 +462,15 @@
             (((1,), (1,)), ((), ())),
             preferred_element_type=jnp.float32,
         )
-        attended[pl.ds(first, block_rows), :] = (summed / total).astype(jnp.bfloat16)
-
-    blocks = heads * token_count // block_rows
-    pl.loop(0, blocks // 2)(attend)
-    z_forward(3, 1)
-    z_forward(4, 1)
-    pl.loop(blocks // 2, blocks)(attend)
-
-    own_rows = hidden_ref.shape[0]
-    result_rows = jnp.concatenate(
-        [attended[head * token_count : (head + 1) * token_count, :] for head in range(heads)],
-        axis=1,
-    )
+        return (summed / total).astype(jnp.bfloat16)
+
+    for half in range(2):
+        attended[half, z] = jnp.concatenate(
+            [attend(half, head) for head in range(heads)], axis=1
+        )
+        z_forward(3 + half, 0)
+
+    width = wo_own.shape[1]
 
     def sib_copy(n):
         return pltpu.make_async_remote_copy(
@@ -496,8 +494,8 @@
 
     def project(n):
         partial[n] = jnp.dot(
-            result_rows, wo_all[n % 2, order[n // 2]], preferred_element_type=jnp.float32
-        ).reshape(2 * CHIPS, own_rows, half_width)
+            attended[n % 2, order[n // 2]], wo_own[...], preferred_element_type=jnp.float32
+        ).reshape(2 * CHIPS, half_own, width)
         for k in range(CHIPS):
             sibling_out[n, k] = partial[n, 2 * k + 1 - core].astype(jnp.bfloat16)
         sib_copy(n).start()
@@ -518,27 +516,56 @@
     order[2] = jnp.where((z == 0) | (z == planes - 1), jnp.where(low, 2, planes - 3), order[2])
     order.append(jnp.where(low, planes - 1, 0))
 
-    slices = 2 * planes
-    for n in range(slices):
-        step = n // 2 - 1
-        if n < 2:
-            loads[8 + n].wait()
-        else:
-            z_last(3 + n % 2, step)
-        if n >= 2 and step + 1 == 1:
-            z_forward(3 + n % 2, 2)
-        project(n)
-        if n > 0:
-            spread_sums(n - 1)
-    spread_sums(slices - 1)
-    for n in range(slices):
+    def home_copy(n, plane):
+        return pltpu.make_async_remote_copy(
+            src_ref=pieces.at[n],
+            dst_ref=out_ref.at[
+                pl.ds(n % 2 * half_own, half_own), pl.ds(pl.multiple_of(z * width, width), width)
+            ],
+            send_sem=home_send.at[n],
+            recv_sem=home_recv.at[n % 2, z],
+            device_id={"gy": plane},
+            device_id_type=MESH,
+        )
+
+    def finish(n):
         total = own_sum[n]
         for flip in range(FLIPS):
             chip_copy(n, flip).wait_recv()
             total += chip_in[n, flip].astype(jnp.float32)
-        column = pl.multiple_of(order[n // 2] * 2 * half_width + n % 2 * half_width, half_width)
-        out_ref[:, pl.ds(column, half_width)] = total.astype(jnp.bfloat16)
-
+        piece = total.astype(jnp.bfloat16)
+        if n < 2:
+            column = pl.multiple_of(z * width, width)
+            out_ref[n * half_own : (n + 1) * half_own, pl.ds(column, width)] = piece
+        else:
+            pieces[n] = piece
+            home_copy(n, order[n // 2]).start()
+
+    slices = 2 * planes
+    loads[8].wait()
+    for pos in range(planes):
+        pair = (2 * pos, 2 * pos + 1)
+        for n in pair:
+            if pos > 0:
+                z_take(3 + n % 2, order[pos])
+            project(n)
+        if pos > 0:
+            for n in pair:
+                finish(n - 2)
+        for n in pair:
+            spread_sums(n)
+    finish(slices - 2)
+    finish(slices - 1)
+    for plane in other_planes:
+        for half in range(2):
+            landed = out_ref.at[
+                pl.ds(half * half_own, half_own),
+                pl.ds(pl.multiple_of(plane * width, width), width),
+            ]
+            pltpu.make_async_copy(landed, landed, home_recv.at[half, plane]).wait()
+
+    for n in range(2, slices):
+        home_copy(n, order[n // 2]).wait_send()
     for kind in range(5):
         for step in range(planes - 1):
             z_wait_send(kind, step)
@@ -553,6 +580,19 @@
         sib_copy(n).wait_send()
         for flip in range(FLIPS):
             chip_copy(n, flip).wait_send()
+
+
+def hand_over(out_ref, key_ref, value_ref, out_to, key_to, value_to, sem):
+    copies = [
+        pltpu.make_async_copy(source, target.at[0], sem.at[slot])
+        for slot, (source, target) in enumerate(
+            [(out_ref, out_to), (key_ref, key_to), (value_ref, value_to)]
+        )
+    ]
+    for copy in copies:
+        copy.start()
+    for copy in copies:
+        copy.wait()
 
 
 def fused(
@@ -595,19 +635,20 @@
             pltpu.VMEM((groups, own_rows, model), bf16),
             pltpu.VMEM((2, planes, depth // 2, columns), bf16),
             pltpu.VMEM((planes, kv_width, depth), bf16),
-            pltpu.VMEM((2, planes, out_rows, width // 2), bf16),
+            pltpu.VMEM((out_rows, width), bf16),
             pltpu.VMEM((groups, page, head_dim), bf16),
             pltpu.VMEM((groups, page, head_dim), bf16),
             pltpu.VMEM((groups, kv_width, span), bf16),
-            pltpu.VMEM((heads * span, head_dim), bf16),
-            pltpu.VMEM((heads * span, head_dim), bf16),
-            pltpu.VMEM((2 * planes, 2 * CHIPS, own_rows, width // 2), f32),
-            pltpu.VMEM((2 * planes, CHIPS, own_rows, width // 2), bf16),
-            pltpu.VMEM((2 * planes, CHIPS, own_rows, width // 2), bf16),
-            pltpu.VMEM((2 * planes, FLIPS, own_rows, width // 2), bf16),
-            pltpu.VMEM((2 * planes, FLIPS, own_rows, width // 2), bf16),
-            pltpu.VMEM((2 * planes, own_rows, width // 2), f32),
-            dma((10,)),
+            pltpu.VMEM((2 * heads, span // 2, head_dim), bf16),
+            pltpu.VMEM((2, planes, span // 2, heads * head_dim), bf16),
+            pltpu.VMEM((2 * planes, 2 * CHIPS, own_rows // 2, width), f32),
+            pltpu.VMEM((2 * planes, CHIPS, own_rows // 2, width), bf16),
+            pltpu.VMEM((2 * planes, CHIPS, own_rows // 2, width), bf16),
+            pltpu.VMEM((2 * planes, FLIPS, own_rows // 2, width), bf16),
+            pltpu.VMEM((2 * planes, FLIPS, own_rows // 2, width), bf16),
+            pltpu.VMEM((2 * planes, own_rows // 2, width), f32),
+            pltpu.VMEM((2 * planes, own_rows // 2, width), bf16),
+            dma((9,)),
             dma((5, planes - 1, 2)),
             dma((5, planes)),
             dma((3, 4 + FLIPS)),
@@ -618,6 +659,8 @@
             dma((2 * planes,)),
             dma((2 * planes, FLIPS)),
             dma((2 * planes, FLIPS)),
+            dma((2 * planes,)),
+            dma((2, planes)),
         ],
         compiler_params=pltpu.CompilerParams(
             collective_id=0, has_side_effects=True, vmem_limit_bytes=64 * 1024 * 1024
@@ -637,7 +680,18 @@
         value_cache[0],
         cache_length,
     )
-    return out[None], new_key[None], new_value[None]
+    results = pl.pallas_call(
+        hand_over,
+        out_shape=tuple(
+            jax.ShapeDtypeStruct((1,) + result.shape, bf16) for result in (out, new_key, new_value)
+        ),
+        in_specs=[hbm] * 3,
+        out_specs=(hbm,) * 3,
+        scratch_shapes=[dma((3,))],
+        compiler_params=pltpu.CompilerParams(vmem_limit_bytes=64 * 1024 * 1024),
+        name="hand_over",
+    )(out, new_key, new_value)
+    return tuple(results)
 
 
 def device_program(mesh, *args):

time: 54.8 us -> 64.8 us (1.18)
  Pallas kernels: 50.2 us -> 63.4 us
  local copies, waits for them, and re-layouts: 3.15 us -> 0 us
    pallas_call x0 -> x1, Pallas kernels: none -> 9.57 us  [fused(): pl.pallas_call(hand_over, out_shape=tuple((jax.ShapeDtypeStruct((1,) + re...]
    pallas_call x1, Pallas kernels: 50.2 us -> 53.8 us  [fused(): pl.pallas_call(functools.partial(fused_kernel, planes), out_shape=(jax.Sh...]
    unnamed x7 -> x0, local copies, waits for them, and re-layouts: 3.15 us -> none
where the time goes in v3:
time: 64.8 us; the launch traced here: 64.7 us
  Pallas kernels  63.4 us (98%)
  between operations  1.29 us (2%)
    pallas_call x1, Pallas kernels, fused(): pl.pallas_call(functools.partial(fused_kernel, planes), out_shape=(jax.Sh...  53.8 us
    pallas_call x1, Pallas kernels, fused(): pl.pallas_call(hand_over, out_shape=tuple((jax.ShapeDtypeStruct((1,) + re...  9.57 us

profile of v3, /device:TPU:0, one launch (start us, length us, event | category | flops | bytes accessed | tf_op | source)
XLA Modules:
  0.0 64.7 jit_solution(1645966027751721840)
XLA Ops:
  1.3 53.8 %attention_layer.1 = (bf16[32,2048]{1,0:T(8,128)(2,1)}, bf16[288,128]{1,0:T(8,128)(2,1)}, bf16[288,128]{1,0:T(8,128)(2,1)}) custom-call(bf16[32,2048]{1,0:T(8,128)(2,1)} %bitcast.6, f32[1,2048]{1,0:T(1,128)} %bitcast.10, f32[1,2048]{1,0:T(1,128)} %bitcast.11, bf16[512,256]{1,0:T(8,128)(2,1)} %wq_ref.1, bf16[32,512]{1,0:T(8,128)(2,1)} %bitcast.9, ...), custom_call_target="tpu_custom_call" | custom-call | flops 1000000000 | bytes 2000000 | tf_op jit(solution)/shard_map/attention_layer/pallas_call | solution.py:622
  55.1 9.6 %hand_over.1 = (bf16[1,32,2048]{2,1,0:T(8,128)(2,1)}, bf16[1,288,128]{2,1,0:T(8,128)(2,1)}, bf16[1,288,128]{2,1,0:T(8,128)(2,1)}) custom-call(bf16[32,2048]{1,0:T(8,128)(2,1)} %get-tuple-element.6.out_ref, bf16[288,128]{1,0:T(8,128)(2,1)} %get-tuple-element.7.key_ref, bf16[288,128]{1,0:T(8,128)(2,1)} %get-tuple-element.8.value_ref), custom_call_target="tpu_custom_call" | custom-call | tf_op jit(solution)/shard_map/hand_over/pallas_call | solution.py:683

commit v4 on v3

--- a/solution.py
+++ b/solution.py
@@ -160,7 +160,6 @@
     keys,
     values,
     new_kv,
-    query_rows,
     attended,
     partial,
     sibling_out,
@@ -205,9 +204,9 @@
     for plane in other_planes:
         pl.semaphore_signal(barrier, inc=1, device_id={"gy": plane}, device_id_type=MESH)
 
-    half_depth = wq_all.shape[2]
-    half_rows = [wq_ref.at[pl.ds(half * half_depth, half_depth)] for half in range(2)]
-    sources = [wkv_ref] + half_rows
+    head_dim = key_ref.shape[1]
+    head_columns = [wq_ref.at[:, pl.ds(head * head_dim, head_dim)] for head in range(2)]
+    sources = [wkv_ref] + head_columns
     buffers = [wkv_all, wq_all.at[0], wq_all.at[1], attended.at[0], attended.at[1]]
     loads = [
         pltpu.make_async_copy(source, target, load_sem.at[slot])
@@ -274,6 +273,14 @@
         def _():
             z_arrived(kind, z + 1 + step)
 
+    def second_start(step):
+        for direction in (1, -1):
+            last = z if direction > 0 else planes - 1 - z
+
+            @pl.when(z_cond(0, direction) & (last == step))
+            def _(direction=direction):
+                z_copy(2, 0, direction, True).start()
+
     def z_take(kind, shard):
         z_arrived(kind, shard)
 
@@ -315,8 +322,9 @@
         for block in [sibling] + far:
             rows_wait(kind, block)
 
-    for kind in range(3):
+    for kind in range(2):
         z_forward(kind, 0)
+    second_start(0)
 
     for slot in range(3):
         loads[slot].wait()
@@ -335,8 +343,10 @@
     z_forward(0, 1)
     z_forward(0, 2)
     z_forward(1, 1)
+    second_start(1)
     rows_forward(0)
-    z_forward(2, 1)
+    z_forward(1, 2)
+    second_start(2)
     rows_finish(0)
     loads[5].wait()
     for step in range(planes - 1):
@@ -344,7 +354,7 @@
 
     tokens = normed[...].reshape(-1, normed.shape[2])
     token_count = tokens.shape[0]
-    depth = 2 * half_depth
+    depth = wq_all.shape[2]
     kv_width = wkv_all.shape[1]
     kv_part = jnp.zeros((kv_width, token_count), jnp.float32)
     for part in range(planes):
@@ -370,16 +380,14 @@
         kv_copy(me, target, slot).start()
 
     rows_forward(1)
-    z_forward(1, 2)
     rows_forward(2)
-    z_forward(2, 2)
+    z_forward(2, 1)
 
     for block in everyone:
         pltpu.make_async_copy(new_kv.at[block], new_kv.at[block], kv_recv.at[block]).wait()
 
     length = length_ref[0]
     page = key_ref.shape[0]
-    head_dim = key_ref.shape[1]
     kv_cols = new_kv[...].reshape(2 * head_dim, token_count)
     offsets = (
         lax.broadcasted_iota(jnp.int32, (page, token_count), 0) + me * page - length
@@ -402,49 +410,34 @@
 
     rows_finish(1)
     rows_finish(2)
-    for half in range(2):
-        loads[6 + half].wait()
+    def queries(head):
+        loads[6 + head].wait()
         for step in range(planes - 1):
-            z_last(1 + half, step)
-
-    heads = wq_all.shape[3] // head_dim
-    query = jnp.zeros((token_count, heads * head_dim), jnp.float32)
-    for part in range(2 * planes):
-        query += jnp.dot(
-            normed[:, :, part * half_depth : (part + 1) * half_depth].reshape(
-                token_count, half_depth
-            ),
-            wq_all[part % 2, part // 2],
-            preferred_element_type=jnp.float32,
-        )
-    query = query.astype(jnp.bfloat16)
-    own_rows = hidden_ref.shape[0]
-    half_own = own_rows // 2
-    half_rows = token_count // 2
-    query = query.reshape(2 * CHIPS, own_rows, heads * head_dim)
-    for half in range(2):
-        rows_of_half = query[:, half * half_own : (half + 1) * half_own].reshape(half_rows, -1)
-        for head in range(heads):
-            query_rows[half * heads + head] = rows_of_half[
-                :, head * head_dim : (head + 1) * head_dim
-            ]
+            z_last(1 + head, step)
+        query = jnp.zeros((token_count, head_dim), jnp.float32)
+        for part in range(planes):
+            query += jnp.dot(
+                normed[:, :, part * depth : (part + 1) * depth].reshape(token_count, depth),
+                wq_all[head, part],
+                preferred_element_type=jnp.float32,
+            )
+        return query.astype(jnp.bfloat16)
 
     cached = keys.shape[0] * page - token_count
-    block_rows = half_rows
+    block_rows = token_count
     scale = head_dim ** (-0.5) * math.log2(math.e)
 
-    def attend(half, head):
-        q = query_rows[half * heads + head]
+    def attend(q):
         old_keys = keys[...].reshape(-1, head_dim)[:cached]
         old_values = values[...].reshape(-1, head_dim)[:cached]
         fresh = new_kv[...].reshape(2 * head_dim, token_count)
-        old_pos = lax.broadcasted_iota(jnp.int32, (block_rows, cached), 1)
+        old_pos = lax.broadcasted_iota(jnp.int32, (1, cached), 1)
+        hidden = jnp.where(old_pos < length, 0.0, NEGATIVE)
         old = lax.dot_general(
             q, old_keys, (((1,), (1,)), ((), ())), preferred_element_type=jnp.float32
         )
-        old = jnp.where(old_pos < length, old * scale, NEGATIVE)
+        old = old * scale + hidden
         row = lax.broadcasted_iota(jnp.int32, (block_rows, token_count), 0)
-        row = row // half_own * own_rows + half * half_own + row % half_own
         col = lax.broadcasted_iota(jnp.int32, (block_rows, token_count), 1)
         new = jnp.dot(q, fresh[:head_dim], preferred_element_type=jnp.float32)
         new = jnp.where(col <= row, new * scale, NEGATIVE)
@@ -464,12 +457,13 @@
         )
         return (summed / total).astype(jnp.bfloat16)
 
-    for half in range(2):
-        attended[half, z] = jnp.concatenate(
-            [attend(half, head) for head in range(heads)], axis=1
-        )
-        z_forward(3 + half, 0)
-
+    for head in range(2):
+        attended[head, z] = attend(queries(head))
+        z_forward(3 + head, 0)
+        if head == 0:
+            z_forward(2, 2)
+
+    own_rows = hidden_ref.shape[0]
     width = wo_own.shape[1]
 
     def sib_copy(n):
@@ -492,10 +486,15 @@
             device_id_type=MESH,
         )
 
+    def head_product(n, head):
+        return jnp.dot(
+            attended[head, order[n]],
+            wo_own[head * head_dim : (head + 1) * head_dim, :],
+            preferred_element_type=jnp.float32,
+        ).reshape(2 * CHIPS, own_rows, width)
+
     def project(n):
-        partial[n] = jnp.dot(
-            attended[n % 2, order[n // 2]], wo_own[...], preferred_element_type=jnp.float32
-        ).reshape(2 * CHIPS, half_own, width)
+        partial[n] += head_product(n, 1)
         for k in range(CHIPS):
             sibling_out[n, k] = partial[n, 2 * k + 1 - core].astype(jnp.bfloat16)
         sib_copy(n).start()
@@ -519,11 +518,9 @@
     def home_copy(n, plane):
         return pltpu.make_async_remote_copy(
             src_ref=pieces.at[n],
-            dst_ref=out_ref.at[
-                pl.ds(n % 2 * half_own, half_own), pl.ds(pl.multiple_of(z * width, width), width)
-            ],
+            dst_ref=out_ref.at[:, pl.ds(pl.multiple_of(z * width, width), width)],
             send_sem=home_send.at[n],
-            recv_sem=home_recv.at[n % 2, z],
+            recv_sem=home_recv.at[z],
             device_id={"gy": plane},
             device_id_type=MESH,
         )
@@ -534,38 +531,31 @@
             chip_copy(n, flip).wait_recv()
             total += chip_in[n, flip].astype(jnp.float32)
         piece = total.astype(jnp.bfloat16)
-        if n < 2:
-            column = pl.multiple_of(z * width, width)
-            out_ref[n * half_own : (n + 1) * half_own, pl.ds(column, width)] = piece
+        if n == 0:
+            out_ref[:, pl.ds(pl.multiple_of(z * width, width), width)] = piece
         else:
             pieces[n] = piece
-            home_copy(n, order[n // 2]).start()
-
-    slices = 2 * planes
+            home_copy(n, order[n]).start()
+
     loads[8].wait()
-    for pos in range(planes):
-        pair = (2 * pos, 2 * pos + 1)
-        for n in pair:
-            if pos > 0:
-                z_take(3 + n % 2, order[pos])
-            project(n)
-        if pos > 0:
-            for n in pair:
-                finish(n - 2)
-        for n in pair:
-            spread_sums(n)
-    finish(slices - 2)
-    finish(slices - 1)
+    for n in range(planes):
+        if n > 0:
+            z_take(3, order[n])
+        partial[n] = head_product(n, 0)
+    for n in range(planes):
+        if n > 0:
+            z_take(4, order[n])
+        project(n)
+        if n > 0:
+            finish(n - 1)
+        spread_sums(n)
+    finish(planes - 1)
     for plane in other_planes:
-        for half in range(2):
-            landed = out_ref.at[
-                pl.ds(half * half_own, half_own),
-                pl.ds(pl.multiple_of(plane * width, width), width),
-            ]
-            pltpu.make_async_copy(landed, landed, home_recv.at[half, plane]).wait()
-
-    for n in range(2, slices):
-        home_copy(n, order[n // 2]).wait_send()
+        landed = out_ref.at[:, pl.ds(pl.multiple_of(plane * width, width), width)]
+        pltpu.make_async_copy(landed, landed, home_recv.at[plane]).wait()
+
+    for n in range(1, planes):
+        home_copy(n, order[n]).wait_send()
     for kind in range(5):
         for step in range(planes - 1):
             z_wait_send(kind, step)
@@ -576,23 +566,16 @@
             row_copy(kind, peers[flip], sibling, 4 + flip).wait_send()
     for slot, target in enumerate(everyone):
         kv_copy(me, target, slot).wait_send()
-    for n in range(slices):
+    for n in range(planes):
         sib_copy(n).wait_send()
         for flip in range(FLIPS):
             chip_copy(n, flip).wait_send()
 
 
-def hand_over(out_ref, key_ref, value_ref, out_to, key_to, value_to, sem):
-    copies = [
-        pltpu.make_async_copy(source, target.at[0], sem.at[slot])
-        for slot, (source, target) in enumerate(
-            [(out_ref, out_to), (key_ref, key_to), (value_ref, value_to)]
-        )
-    ]
-    for copy in copies:
-        copy.start()
-    for copy in copies:
-        copy.wait()
+def hand_over(out_ref, key_ref, value_ref, out_to, key_to, value_to):
+    out_to[0] = out_ref[...]
+    key_to[0] = key_ref[...]
+    value_to[0] = value_ref[...]
 
 
 def fused(
@@ -633,21 +616,20 @@
             pltpu.VMEM((1, model), f32),
             pltpu.VMEM((1, model), f32),
             pltpu.VMEM((groups, own_rows, model), bf16),
-            pltpu.VMEM((2, planes, depth // 2, columns), bf16),
+            pltpu.VMEM((heads, planes, depth, head_dim), bf16),
             pltpu.VMEM((planes, kv_width, depth), bf16),
             pltpu.VMEM((out_rows, width), bf16),
             pltpu.VMEM((groups, page, head_dim), bf16),
             pltpu.VMEM((groups, page, head_dim), bf16),
             pltpu.VMEM((groups, kv_width, span), bf16),
-            pltpu.VMEM((2 * heads, span // 2, head_dim), bf16),
-            pltpu.VMEM((2, planes, span // 2, heads * head_dim), bf16),
-            pltpu.VMEM((2 * planes, 2 * CHIPS, own_rows // 2, width), f32),
-            pltpu.VMEM((2 * planes, CHIPS, own_rows // 2, width), bf16),
-            pltpu.VMEM((2 * planes, CHIPS, own_rows // 2, width), bf16),
-            pltpu.VMEM((2 * planes, FLIPS, own_rows // 2, width), bf16),
-            pltpu.VMEM((2 * planes, FLIPS, own_rows // 2, width), bf16),
-            pltpu.VMEM((2 * planes, own_rows // 2, width), f32),
-            pltpu.VMEM((2 * planes, own_rows // 2, width), bf16),
+            pltpu.VMEM((heads, planes, span, head_dim), bf16),
+            pltpu.VMEM((planes, 2 * CHIPS, own_rows, width), f32),
+            pltpu.VMEM((planes, CHIPS, own_rows, width), bf16),
+            pltpu.VMEM((planes, CHIPS, own_rows, width), bf16),
+            pltpu.VMEM((planes, FLIPS, own_rows, width), bf16),
+            pltpu.VMEM((planes, FLIPS, own_rows, width), bf16),
+            pltpu.VMEM((planes, own_rows, width), f32),
+            pltpu.VMEM((planes, own_rows, width), bf16),
             dma((9,)),
             dma((5, planes - 1, 2)),
             dma((5, planes)),
@@ -655,12 +637,12 @@
             dma((3, groups)),
             dma((groups - 1,)),
             dma((groups,)),
-            dma((2 * planes,)),
-            dma((2 * planes,)),
-            dma((2 * planes, FLIPS)),
-            dma((2 * planes, FLIPS)),
-            dma((2 * planes,)),
-            dma((2, planes)),
+            dma((planes,)),
+            dma((planes,)),
+            dma((planes, FLIPS)),
+            dma((planes, FLIPS)),
+            dma((planes,)),
+            dma((planes,)),
         ],
         compiler_params=pltpu.CompilerParams(
             collective_id=0, has_side_effects=True, vmem_limit_bytes=64 * 1024 * 1024
@@ -685,9 +667,8 @@
         out_shape=tuple(
             jax.ShapeDtypeStruct((1,) + result.shape, bf16) for result in (out, new_key, new_value)
         ),
-        in_specs=[hbm] * 3,
-        out_specs=(hbm,) * 3,
-        scratch_shapes=[dma((3,))],
+        in_specs=[vmem] * 3,
+        out_specs=(vmem,) * 3,
         compiler_params=pltpu.CompilerParams(vmem_limit_bytes=64 * 1024 * 1024),
         name="hand_over",
     )(out, new_key, new_value)

time: 64.8 us -> 59.1 us (0.912)
  Pallas kernels: 63.4 us -> 57.7 us
    pallas_call x1, Pallas kernels: 9.57 us -> 1.69 us  [fused(): pl.pallas_call(hand_over, out_shape=tuple((jax.ShapeDtypeStruct((1,) + re...]
    pallas_call x1, Pallas kernels: 53.8 us -> 56 us  [fused(): pl.pallas_call(functools.partial(fused_kernel, planes), out_shape=(jax.Sh...]
where the time goes in v4:
time: 59.1 us; the launch traced here: 58.9 us
  Pallas kernels  57.7 us (98%)
  between operations  1.29 us (2%)
    pallas_call x1, Pallas kernels, fused(): pl.pallas_call(functools.partial(fused_kernel, planes), out_shape=(jax.Sh...  56 us
    pallas_call x1, Pallas kernels, fused(): pl.pallas_call(hand_over, out_shape=tuple((jax.ShapeDtypeStruct((1,) + re...  1.69 us

profile of v4, /device:TPU:0, one launch (start us, length us, event | category | flops | bytes accessed | tf_op | source)
XLA Modules:
  0.0 58.9 jit_solution(13855994599637658906)
XLA Ops:
  1.3 56.0 %attention_layer.1 = (bf16[32,2048]{1,0:T(8,128)(2,1)}, bf16[288,128]{1,0:T(8,128)(2,1)}, bf16[288,128]{1,0:T(8,128)(2,1)}) custom-call(bf16[32,2048]{1,0:T(8,128)(2,1)} %bitcast.6, f32[1,2048]{1,0:T(1,128)} %bitcast.10, f32[1,2048]{1,0:T(1,128)} %bitcast.11, bf16[512,256]{1,0:T(8,128)(2,1)} %wq_ref.1, bf16[32,512]{1,0:T(8,128)(2,1)} %bitcast.9, ...), custom_call_target="tpu_custom_call" | custom-call | flops 1000000000 | bytes 2000000 | tf_op jit(solution)/shard_map/attention_layer/pallas_call | solution.py:605
  57.2 1.7 %hand_over.1 = (bf16[1,32,2048]{2,1,0:T(8,128)(2,1)}, bf16[1,288,128]{2,1,0:T(8,128)(2,1)}, bf16[1,288,128]{2,1,0:T(8,128)(2,1)}) custom-call(bf16[32,2048]{1,0:T(8,128)(2,1)} %get-tuple-element.6.out_ref, bf16[288,128]{1,0:T(8,128)(2,1)} %get-tuple-element.7.key_ref, bf16[288,128]{1,0:T(8,128)(2,1)} %get-tuple-element.8.value_ref), custom_call_target="tpu_custom_call" | custom-call | tf_op jit(solution)/shard_map/hand_over/pallas_call | solution.py:665

commit v5 on v4

--- a/solution.py
+++ b/solution.py
@@ -161,6 +161,9 @@
     values,
     new_kv,
     attended,
+    keys_turned,
+    hidden_row,
+    scores,
     partial,
     sibling_out,
     sibling_in,
@@ -424,38 +427,60 @@
         return query.astype(jnp.bfloat16)
 
     cached = keys.shape[0] * page - token_count
-    block_rows = token_count
+    chunk = token_count
+    chunks = cached // chunk
     scale = head_dim ** (-0.5) * math.log2(math.e)
+    lanes = 128
+    keys_turned[...] = (
+        keys[...].reshape(-1, head_dim)[:cached].astype(jnp.float32).T.astype(jnp.bfloat16)
+    )
+    old_pos = lax.broadcasted_iota(jnp.int32, hidden_row.shape, 1)
+    hidden_row[...] = jnp.where(old_pos < length, 0.0, NEGATIVE)
 
     def attend(q):
-        old_keys = keys[...].reshape(-1, head_dim)[:cached]
-        old_values = values[...].reshape(-1, head_dim)[:cached]
-        fresh = new_kv[...].reshape(2 * head_dim, token_count)
-        old_pos = lax.broadcasted_iota(jnp.int32, (1, cached), 1)
-        hidden = jnp.where(old_pos < length, 0.0, NEGATIVE)
-        old = lax.dot_general(
-            q, old_keys, (((1,), (1,)), ((), ())), preferred_element_type=jnp.float32
-        )
-        old = old * scale + hidden
-        row = lax.broadcasted_iota(jnp.int32, (block_rows, token_count), 0)
-        col = lax.broadcasted_iota(jnp.int32, (block_rows, token_count), 1)
-        new = jnp.dot(q, fresh[:head_dim], preferred_element_type=jnp.float32)
-        new = jnp.where(col <= row, new * scale, NEGATIVE)
-        top = jnp.maximum(
-            jnp.max(old, axis=1, keepdims=True), jnp.max(new, axis=1, keepdims=True)
-        )
-        old = jnp.exp2(old - top)
-        new = jnp.exp2(new - top)
-        total = jnp.sum(old, axis=1, keepdims=True) + jnp.sum(new, axis=1, keepdims=True)
-        summed = jnp.dot(
-            old.astype(jnp.bfloat16), old_values, preferred_element_type=jnp.float32
-        ) + lax.dot_general(
-            new.astype(jnp.bfloat16),
-            fresh[head_dim:],
-            (((1,), (1,)), ((), ())),
-            preferred_element_type=jnp.float32,
-        )
-        return (summed / total).astype(jnp.bfloat16)
+        running = None
+        for c in range(chunks + 1):
+            if c < chunks:
+                part = jnp.dot(
+                    q,
+                    keys_turned[:, c * chunk : (c + 1) * chunk],
+                    preferred_element_type=jnp.float32,
+                )
+                part = part * scale + hidden_row[:1, c * chunk : (c + 1) * chunk]
+            else:
+                part = jnp.dot(
+                    q,
+                    new_kv[...].reshape(2 * head_dim, token_count)[:head_dim],
+                    preferred_element_type=jnp.float32,
+                )
+                row = lax.broadcasted_iota(jnp.int32, part.shape, 0) % token_count
+                col = lax.broadcasted_iota(jnp.int32, part.shape, 1)
+                part = jnp.where(col <= row, part * scale, NEGATIVE)
+            scores[c] = part
+            for first in range(0, chunk, lanes):
+                piece = part[:, first : first + lanes]
+                running = piece if running is None else jnp.maximum(running, piece)
+        top = jnp.max(running, axis=1, keepdims=True)
+        total = jnp.zeros((q.shape[0], lanes), jnp.float32)
+        summed = jnp.zeros((q.shape[0], head_dim), jnp.float32)
+        for c in range(chunks + 1):
+            probs = jnp.exp2(scores[c] - top)
+            for first in range(0, chunk, lanes):
+                total += probs[:, first : first + lanes]
+            if c < chunks:
+                summed += jnp.dot(
+                    probs.astype(jnp.bfloat16),
+                    values[...].reshape(-1, head_dim)[c * chunk : (c + 1) * chunk],
+                    preferred_element_type=jnp.float32,
+                )
+            else:
+                summed += lax.dot_general(
+                    probs.astype(jnp.bfloat16),
+                    new_kv[...].reshape(2 * head_dim, token_count)[head_dim:],
+                    (((1,), (1,)), ((), ())),
+                    preferred_element_type=jnp.float32,
+                )
+        return (summed / jnp.sum(total, axis=1, keepdims=True)).astype(jnp.bfloat16)
 
     for head in range(2):
         attended[head, z] = attend(queries(head))
@@ -623,6 +648,9 @@
             pltpu.VMEM((groups, page, head_dim), bf16),
             pltpu.VMEM((groups, kv_width, span), bf16),
             pltpu.VMEM((heads, planes, span, head_dim), bf16),
+            pltpu.VMEM((head_dim, groups * page - span), bf16),
+            pltpu.VMEM((8, groups * page - span), f32),
+            pltpu.VMEM((groups * page // span, span, span), f32),
             pltpu.VMEM((planes, 2 * CHIPS, own_rows, width), f32),
             pltpu.VMEM((planes, CHIPS, own_rows, width), bf16),
             pltpu.VMEM((planes, CHIPS, own_rows, width), bf16),

time: 59.1 us -> 58.8 us (level)
  no operation moved by 1% of the time
where the time goes in v5:
time: 58.8 us; the launch traced here: 58.6 us
  Pallas kernels  57.3 us (97%)
  between operations  1.29 us (2%)
    pallas_call x1, Pallas kernels, fused(): pl.pallas_call(functools.partial(fused_kernel, planes), out_shape=(jax.Sh...  55.6 us
    pallas_call x1, Pallas kernels, fused(): pl.pallas_call(hand_over, out_shape=tuple((jax.ShapeDtypeStruct((1,) + re...  1.69 us

profile of v5, /device:TPU:0, one launch (start us, length us, event | category | flops | bytes accessed | tf_op | source)
XLA Modules:
  0.0 58.6 jit_solution(18261248535942381143)
XLA Ops:
  1.3 55.6 %attention_layer.1 = (bf16[32,2048]{1,0:T(8,128)(2,1)}, bf16[288,128]{1,0:T(8,128)(2,1)}, bf16[288,128]{1,0:T(8,128)(2,1)}) custom-call(bf16[32,2048]{1,0:T(8,128)(2,1)} %bitcast.6, f32[1,2048]{1,0:T(1,128)} %bitcast.10, f32[1,2048]{1,0:T(1,128)} %bitcast.11, bf16[512,256]{1,0:T(8,128)(2,1)} %wq_ref.1, bf16[32,512]{1,0:T(8,128)(2,1)} %bitcast.9, ...), custom_call_target="tpu_custom_call" | custom-call | flops 1000000000 | bytes 2000000 | tf_op jit(solution)/shard_map/attention_layer/pallas_call | solution.py:630
  56.9 1.7 %hand_over.1 = (bf16[1,32,2048]{2,1,0:T(8,128)(2,1)}, bf16[1,288,128]{2,1,0:T(8,128)(2,1)}, bf16[1,288,128]{2,1,0:T(8,128)(2,1)}) custom-call(bf16[32,2048]{1,0:T(8,128)(2,1)} %get-tuple-element.6.out_ref, bf16[288,128]{1,0:T(8,128)(2,1)} %get-tuple-element.7.key_ref, bf16[288,128]{1,0:T(8,128)(2,1)} %get-tuple-element.8.value_ref), custom_call_target="tpu_custom_call" | custom-call | tf_op jit(solution)/shard_map/hand_over/pallas_call | solution.py:693

commit v6 on v5

--- a/solution.py
+++ b/solution.py
@@ -383,8 +383,9 @@
         kv_copy(me, target, slot).start()
 
     rows_forward(1)
+    z_forward(2, 1)
     rows_forward(2)
-    z_forward(2, 1)
+    z_forward(2, 2)
 
     for block in everyone:
         pltpu.make_async_copy(new_kv.at[block], new_kv.at[block], kv_recv.at[block]).wait()
@@ -485,9 +486,6 @@
     for head in range(2):
         attended[head, z] = attend(queries(head))
         z_forward(3 + head, 0)
-        if head == 0:
-            z_forward(2, 2)
-
     own_rows = hidden_ref.shape[0]
     width = wo_own.shape[1]
 
@@ -519,7 +517,7 @@
         ).reshape(2 * CHIPS, own_rows, width)
 
     def project(n):
-        partial[n] += head_product(n, 1)
+        partial[n] = head_product(n, 0) + head_product(n, 1)
         for k in range(CHIPS):
             sibling_out[n, k] = partial[n, 2 * k + 1 - core].astype(jnp.bfloat16)
         sib_copy(n).start()
@@ -566,14 +564,14 @@
     for n in range(planes):
         if n > 0:
             z_take(3, order[n])
-        partial[n] = head_product(n, 0)
-    for n in range(planes):
-        if n > 0:
             z_take(4, order[n])
         project(n)
         if n > 0:
-            finish(n - 1)
-        spread_sums(n)
+            spread_sums(n - 1)
+        if n > 1:
+            finish(n - 2)
+    spread_sums(planes - 1)
+    finish(planes - 2)
     finish(planes - 1)
     for plane in other_planes:
         landed = out_ref.at[:, pl.ds(pl.multiple_of(plane * width, width), width)]

time: 58.8 us -> 55.5 us (0.944)
  Pallas kernels: 57.3 us -> 54.1 us
    pallas_call x1, Pallas kernels: 55.6 us -> 52.4 us  [fused(): pl.pallas_call(functools.partial(fused_kernel, planes), out_shape=(jax.Sh...]
where the time goes in v6:
time: 55.5 us; the launch traced here: 55.4 us
  Pallas kernels  54.1 us (97%)
  between operations  1.29 us (2%)
    pallas_call x1, Pallas kernels, fused(): pl.pallas_call(functools.partial(fused_kernel, planes), out_shape=(jax.Sh...  52.4 us
    pallas_call x1, Pallas kernels, fused(): pl.pallas_call(hand_over, out_shape=tuple((jax.ShapeDtypeStruct((1,) + re...  1.69 us

profile of v6, /device:TPU:0, one launch (start us, length us, event | category | flops | bytes accessed | tf_op | source)
XLA Modules:
  0.0 55.4 jit_solution(5462740342576394891)
XLA Ops:
  1.3 52.4 %attention_layer.1 = (bf16[32,2048]{1,0:T(8,128)(2,1)}, bf16[288,128]{1,0:T(8,128)(2,1)}, bf16[288,128]{1,0:T(8,128)(2,1)}) custom-call(bf16[32,2048]{1,0:T(8,128)(2,1)} %bitcast.6, f32[1,2048]{1,0:T(1,128)} %bitcast.10, f32[1,2048]{1,0:T(1,128)} %bitcast.11, bf16[512,256]{1,0:T(8,128)(2,1)} %wq_ref.1, bf16[32,512]{1,0:T(8,128)(2,1)} %bitcast.9, ...), custom_call_target="tpu_custom_call" | custom-call | flops 1000000000 | bytes 2000000 | tf_op jit(solution)/shard_map/attention_layer/pallas_call | solution.py:628
  53.7 1.7 %hand_over.1 = (bf16[1,32,2048]{2,1,0:T(8,128)(2,1)}, bf16[1,288,128]{2,1,0:T(8,128)(2,1)}, bf16[1,288,128]{2,1,0:T(8,128)(2,1)}) custom-call(bf16[32,2048]{1,0:T(8,128)(2,1)} %get-tuple-element.6.out_ref, bf16[288,128]{1,0:T(8,128)(2,1)} %get-tuple-element.7.key_ref, bf16[288,128]{1,0:T(8,128)(2,1)} %get-tuple-element.8.value_ref), custom_call_target="tpu_custom_call" | custom-call | tf_op jit(solution)/shard_map/hand_over/pallas_call | solution.py:691

commit v7 on v2

--- a/solution.py
+++ b/solution.py
@@ -162,6 +162,9 @@
     new_kv,
     query_rows,
     attended,
+    keys_turned,
+    hidden_row,
+    scores,
     partial,
     sibling_out,
     sibling_in,
@@ -299,7 +302,7 @@
         )
 
     def rows_start(kind):
-        for slot, target in enumerate(peers + [sibling]):
+        for slot, target in enumerate((peers[0], peers[1], sibling)):
             row_copy(kind, me, target, slot).start()
 
     def rows_wait(kind, block):
@@ -307,10 +310,22 @@
             gathered[kind].at[block], gathered[kind].at[block], rows_recv.at[kind, block]
         ).wait()
 
+    def across(kind):
+        return (0, 1) if kind == 0 else (1, 0)
+
     def rows_forward(kind):
-        for flip in range(FLIPS):
-            rows_wait(kind, peers[flip])
-            row_copy(kind, peers[flip], sibling, 4 + flip).start()
+        first, second = across(kind)
+        rows_wait(kind, peers[first])
+        row_copy(kind, peers[first], peers[second], 3).start()
+        if kind == 0:
+            for cache in (1, 2):
+                loads[cache + 2].wait()
+                rows_start(cache)
+        row_copy(kind, peers[first], sibling, 4).start()
+        rows_wait(kind, peers[second])
+        row_copy(kind, peers[second], sibling, 5).start()
+        rows_wait(kind, peers[2])
+        row_copy(kind, peers[2], sibling, 6).start()
 
     def rows_finish(kind):
         for block in [sibling] + far:
@@ -330,9 +345,6 @@
         centred * lax.rsqrt(spread + 1e-05) * gain_in[...] + bias_in[...]
     ).astype(jnp.bfloat16)
     rows_start(0)
-    for kind in (1, 2):
-        loads[kind + 2].wait()
-        rows_start(kind)
 
     z_forward(0, 1)
     z_forward(0, 2)
@@ -428,45 +440,67 @@
         ]
 
     cached = keys.shape[0] * page - token_count
-    block_rows = 128
+    chunk = token_count
+    chunks = cached // chunk
     scale = head_dim ** (-0.5) * math.log2(math.e)
-
-    def attend(start):
-        first = pl.multiple_of(start * block_rows, block_rows)
-        q = query_rows[pl.ds(first, block_rows), :]
-        old_keys = keys[...].reshape(-1, head_dim)[:cached]
-        old_values = values[...].reshape(-1, head_dim)[:cached]
-        fresh = new_kv[...].reshape(2 * head_dim, token_count)
-        old_pos = lax.broadcasted_iota(jnp.int32, (block_rows, cached), 1)
-        old = lax.dot_general(
-            q, old_keys, (((1,), (1,)), ((), ())), preferred_element_type=jnp.float32
-        )
-        old = jnp.where(old_pos < length, old * scale, NEGATIVE)
-        row = lax.broadcasted_iota(jnp.int32, (block_rows, token_count), 0) + first % token_count
-        col = lax.broadcasted_iota(jnp.int32, (block_rows, token_count), 1)
-        new = jnp.dot(q, fresh[:head_dim], preferred_element_type=jnp.float32)
-        new = jnp.where(col <= row, new * scale, NEGATIVE)
-        top = jnp.maximum(
-            jnp.max(old, axis=1, keepdims=True), jnp.max(new, axis=1, keepdims=True)
-        )
-        old = jnp.exp2(old - top)
-        new = jnp.exp2(new - top)
-        total = jnp.sum(old, axis=1, keepdims=True) + jnp.sum(new, axis=1, keepdims=True)
-        summed = jnp.dot(
-            old.astype(jnp.bfloat16), old_values, preferred_element_type=jnp.float32
-        ) + lax.dot_general(
-            new.astype(jnp.bfloat16),
-            fresh[head_dim:],
-            (((1,), (1,)), ((), ())),
-            preferred_element_type=jnp.float32,
-        )
-        attended[pl.ds(first, block_rows), :] = (summed / total).astype(jnp.bfloat16)
-
-    blocks = heads * token_count // block_rows
-    pl.loop(0, blocks // 2)(attend)
-    z_forward(3, 1)
-    z_forward(4, 1)
-    pl.loop(blocks // 2, blocks)(attend)
+    lanes = 128
+    keys_turned[...] = (
+        keys[...].reshape(-1, head_dim)[:cached].astype(jnp.float32).T.astype(jnp.bfloat16)
+    )
+    old_pos = lax.broadcasted_iota(jnp.int32, hidden_row.shape, 1)
+    hidden_row[...] = jnp.where(old_pos < length, 0.0, NEGATIVE)
+
+    def attend(q):
+        running = None
+        for c in range(chunks + 1):
+            if c < chunks:
+                part = jnp.dot(
+                    q,
+                    keys_turned[:, c * chunk : (c + 1) * chunk],
+                    preferred_element_type=jnp.float32,
+                )
+                part = part * scale + hidden_row[:1, c * chunk : (c + 1) * chunk]
+            else:
+                part = jnp.dot(
+                    q,
+                    new_kv[...].reshape(2 * head_dim, token_count)[:head_dim],
+                    preferred_element_type=jnp.float32,
+                )
+                row = lax.broadcasted_iota(jnp.int32, part.shape, 0) % token_count
+                col = lax.broadcasted_iota(jnp.int32, part.shape, 1)
+                part = jnp.where(col <= row, part * scale, NEGATIVE)
+            scores[c] = part
+            for first in range(0, chunk, lanes):
+                piece = part[:, first : first + lanes]
+                running = piece if running is None else jnp.maximum(running, piece)
+        top = jnp.max(running, axis=1, keepdims=True)
+        total = jnp.zeros((q.shape[0], lanes), jnp.float32)
+        summed = jnp.zeros((q.shape[0], head_dim), jnp.float32)
+        for c in range(chunks + 1):
+            probs = jnp.exp2(scores[c] - top)
+            for first in range(0, chunk, lanes):
+                total += probs[:, first : first + lanes]
+            if c < chunks:
+                summed += jnp.dot(
+                    probs.astype(jnp.bfloat16),
+                    values[...].reshape(-1, head_dim)[c * chunk : (c + 1) * chunk],
+                    preferred_element_type=jnp.float32,
+                )
+            else:
+                summed += lax.dot_general(
+                    probs.astype(jnp.bfloat16),
+                    new_kv[...].reshape(2 * head_dim, token_count)[head_dim:],
+                    (((1,), (1,)), ((), ())),
+                    preferred_element_type=jnp.float32,
+                )
+        return (summed / jnp.sum(total, axis=1, keepdims=True)).astype(jnp.bfloat16)
+
+    for head in range(heads):
+        head_rows = slice(head * token_count, (head + 1) * token_count)
+        attended[head_rows, :] = attend(query_rows[head_rows, :])
+        if head == 0:
+            z_forward(3, 1)
+            z_forward(4, 1)
 
     own_rows = hidden_ref.shape[0]
     result_rows = jnp.concatenate(
@@ -543,16 +577,24 @@
         for step in range(planes - 1):
             z_wait_send(kind, step)
     for kind in range(3):
-        for slot, target in enumerate(peers + [sibling]):
+        first, second = across(kind)
+        for slot, target in enumerate((peers[0], peers[1], sibling)):
             row_copy(kind, me, target, slot).wait_send()
-        for flip in range(FLIPS):
-            row_copy(kind, peers[flip], sibling, 4 + flip).wait_send()
+        row_copy(kind, peers[first], peers[second], 3).wait_send()
+        for slot, flip in enumerate((first, second, 2)):
+            row_copy(kind, peers[flip], sibling, 4 + slot).wait_send()
     for slot, target in enumerate(everyone):
         kv_copy(me, target, slot).wait_send()
     for n in range(slices):
         sib_copy(n).wait_send()
         for flip in range(FLIPS):
             chip_copy(n, flip).wait_send()
+
+
+def hand_over(out_ref, key_ref, value_ref, out_to, key_to, value_to):
+    out_to[0] = out_ref[...]
+    key_to[0] = key_ref[...]
+    value_to[0] = value_ref[...]
 
 
 def fused(
@@ -601,6 +643,9 @@
             pltpu.VMEM((groups, kv_width, span), bf16),
             pltpu.VMEM((heads * span, head_dim), bf16),
             pltpu.VMEM((heads * span, head_dim), bf16),
+            pltpu.VMEM((head_dim, groups * page - span), bf16),
+            pltpu.VMEM((8, groups * page - span), f32),
+            pltpu.VMEM((groups * page // span, span, span), f32),
             pltpu.VMEM((2 * planes, 2 * CHIPS, own_rows, width // 2), f32),
             pltpu.VMEM((2 * planes, CHIPS, own_rows, width // 2), bf16),
             pltpu.VMEM((2 * planes, CHIPS, own_rows, width // 2), bf16),
@@ -637,7 +682,17 @@
         value_cache[0],
         cache_length,
     )
-    return out[None], new_key[None], new_value[None]
+    results = pl.pallas_call(
+        hand_over,
+        out_shape=tuple(
+            jax.ShapeDtypeStruct((1,) + result.shape, bf16) for result in (out, new_key, new_value)
+        ),
+        in_specs=[vmem] * 3,
+        out_specs=(vmem,) * 3,
+        compiler_params=pltpu.CompilerParams(vmem_limit_bytes=64 * 1024 * 1024),
+        name="hand_over",
+    )(out, new_key, new_value)
+    return tuple(results)
 
 
 def device_program(mesh, *args):

time: 54.8 us -> 60.4 us (1.10)
  Pallas kernels: 50.2 us -> 59 us
  local copies, waits for them, and re-layouts: 3.15 us -> 0 us
    pallas_call x1, Pallas kernels: 50.2 us -> 57.3 us  [fused(): pl.pallas_call(functools.partial(fused_kernel, planes), out_shape=(jax.Sh...]
    unnamed x7 -> x0, local copies, waits for them, and re-layouts: 3.15 us -> none
    pallas_call x0 -> x1, Pallas kernels: none -> 1.69 us  [fused(): pl.pallas_call(hand_over, out_shape=tuple((jax.ShapeDtypeStruct((1,) + re...]
where the time goes in v7:
time: 60.4 us; the launch traced here: 60.3 us
  Pallas kernels  59 us (98%)
  between operations  1.29 us (2%)
    pallas_call x1, Pallas kernels, fused(): pl.pallas_call(functools.partial(fused_kernel, planes), out_shape=(jax.Sh...  57.3 us
    pallas_call x1, Pallas kernels, fused(): pl.pallas_call(hand_over, out_shape=tuple((jax.ShapeDtypeStruct((1,) + re...  1.69 us

profile of v7, /device:TPU:0, one launch (start us, length us, event | category | flops | bytes accessed | tf_op | source)
XLA Modules:
  0.0 60.3 jit_solution(17933571369477523761)
XLA Ops:
  1.3 57.3 %attention_layer.1 = (bf16[32,2048]{1,0:T(8,128)(2,1)}, bf16[288,128]{1,0:T(8,128)(2,1)}, bf16[288,128]{1,0:T(8,128)(2,1)}) custom-call(bf16[32,2048]{1,0:T(8,128)(2,1)} %bitcast.6, f32[1,2048]{1,0:T(1,128)} %bitcast.10, f32[1,2048]{1,0:T(1,128)} %bitcast.11, bf16[512,256]{1,0:T(8,128)(2,1)} %wq_ref.1, bf16[32,512]{1,0:T(8,128)(2,1)} %bitcast.9, ...), custom_call_target="tpu_custom_call" | custom-call | flops 1000000000 | bytes 2000000 | tf_op jit(solution)/shard_map/attention_layer/pallas_call | solution.py:624
  58.6 1.7 %hand_over.1 = (bf16[1,32,2048]{2,1,0:T(8,128)(2,1)}, bf16[1,288,128]{2,1,0:T(8,128)(2,1)}, bf16[1,288,128]{2,1,0:T(8,128)(2,1)}) custom-call(bf16[32,2048]{1,0:T(8,128)(2,1)} %get-tuple-element.6.out_ref, bf16[288,128]{1,0:T(8,128)(2,1)} %get-tuple-element.7.key_ref, bf16[288,128]{1,0:T(8,128)(2,1)} %get-tuple-element.8.value_ref), custom_call_target="tpu_custom_call" | custom-call | tf_op jit(solution)/shard_map/hand_over/pallas_call | solution.py:685

commit v8 on v7

--- a/solution.py
+++ b/solution.py
@@ -302,7 +302,7 @@
         )
 
     def rows_start(kind):
-        for slot, target in enumerate((peers[0], peers[1], sibling)):
+        for slot, target in enumerate(peers + [sibling]):
             row_copy(kind, me, target, slot).start()
 
     def rows_wait(kind, block):
@@ -310,22 +310,10 @@
             gathered[kind].at[block], gathered[kind].at[block], rows_recv.at[kind, block]
         ).wait()
 
-    def across(kind):
-        return (0, 1) if kind == 0 else (1, 0)
-
     def rows_forward(kind):
-        first, second = across(kind)
-        rows_wait(kind, peers[first])
-        row_copy(kind, peers[first], peers[second], 3).start()
-        if kind == 0:
-            for cache in (1, 2):
-                loads[cache + 2].wait()
-                rows_start(cache)
-        row_copy(kind, peers[first], sibling, 4).start()
-        rows_wait(kind, peers[second])
-        row_copy(kind, peers[second], sibling, 5).start()
-        rows_wait(kind, peers[2])
-        row_copy(kind, peers[2], sibling, 6).start()
+        for flip in range(FLIPS):
+            rows_wait(kind, peers[flip])
+            row_copy(kind, peers[flip], sibling, 4 + flip).start()
 
     def rows_finish(kind):
         for block in [sibling] + far:
@@ -335,6 +323,8 @@
         z_forward(kind, 0)
     out_start(0)
 
+    loads[3].wait()
+    rows_start(1)
     for slot in range(3):
         loads[slot].wait()
     rows = hidden_in[...].astype(jnp.float32)
@@ -345,6 +335,8 @@
         centred * lax.rsqrt(spread + 1e-05) * gain_in[...] + bias_in[...]
     ).astype(jnp.bfloat16)
     rows_start(0)
+    loads[4].wait()
+    rows_start(2)
 
     z_forward(0, 1)
     z_forward(0, 2)
@@ -384,11 +376,11 @@
     for slot, target in enumerate(everyone):
         kv_copy(me, target, slot).start()
 
-    rows_forward(1)
     z_forward(1, 2)
-    rows_forward(2)
     z_forward(2, 2)
     out_start(2)
+    rows_forward(1)
+    rows_forward(2)
 
     for block in everyone:
         pltpu.make_async_copy(new_kv.at[block], new_kv.at[block], kv_recv.at[block]).wait()
@@ -577,12 +569,10 @@
         for step in range(planes - 1):
             z_wait_send(kind, step)
     for kind in range(3):
-        first, second = across(kind)
-        for slot, target in enumerate((peers[0], peers[1], sibling)):
+        for slot, target in enumerate(peers + [sibling]):
             row_copy(kind, me, target, slot).wait_send()
-        row_copy(kind, peers[first], peers[second], 3).wait_send()
-        for slot, flip in enumerate((first, second, 2)):
-            row_copy(kind, peers[flip], sibling, 4 + slot).wait_send()
+        for flip in range(FLIPS):
+            row_copy(kind, peers[flip], sibling, 4 + flip).wait_send()
     for slot, target in enumerate(everyone):
         kv_copy(me, target, slot).wait_send()
     for n in range(slices):

time: 60.4 us -> 53.3 us (0.88)
  Pallas kernels: 59 us -> 51.9 us
    pallas_call x1, Pallas kernels: 57.3 us -> 50.2 us  [fused(): pl.pallas_call(functools.partial(fused_kernel, planes), out_shape=(jax.Sh...]
where the time goes in v8:
time: 53.3 us; the launch traced here: 53.1 us
  Pallas kernels  51.9 us (97%)
  between operations  1.29 us (2%)
    pallas_call x1, Pallas kernels, fused(): pl.pallas_call(functools.partial(fused_kernel, planes), out_shape=(jax.Sh...  50.2 us
    pallas_call x1, Pallas kernels, fused(): pl.pallas_call(hand_over, out_shape=tuple((jax.ShapeDtypeStruct((1,) + re...  1.69 us

profile of v8, /device:TPU:0, one launch (start us, length us, event | category | flops | bytes accessed | tf_op | source)
XLA Modules:
  0.0 53.1 jit_solution(3249475806134009291)
XLA Ops:
  1.3 50.2 %attention_layer.1 = (bf16[32,2048]{1,0:T(8,128)(2,1)}, bf16[288,128]{1,0:T(8,128)(2,1)}, bf16[288,128]{1,0:T(8,128)(2,1)}) custom-call(bf16[32,2048]{1,0:T(8,128)(2,1)} %bitcast.6, f32[1,2048]{1,0:T(1,128)} %bitcast.10, f32[1,2048]{1,0:T(1,128)} %bitcast.11, bf16[512,256]{1,0:T(8,128)(2,1)} %wq_ref.1, bf16[32,512]{1,0:T(8,128)(2,1)} %bitcast.9, ...), custom_call_target="tpu_custom_call" | custom-call | flops 1000000000 | bytes 2000000 | tf_op jit(solution)/shard_map/attention_layer/pallas_call | solution.py:614
  51.5 1.7 %hand_over.1 = (bf16[1,32,2048]{2,1,0:T(8,128)(2,1)}, bf16[1,288,128]{2,1,0:T(8,128)(2,1)}, bf16[1,288,128]{2,1,0:T(8,128)(2,1)}) custom-call(bf16[32,2048]{1,0:T(8,128)(2,1)} %get-tuple-element.6.out_ref, bf16[288,128]{1,0:T(8,128)(2,1)} %get-tuple-element.7.key_ref, bf16[288,128]{1,0:T(8,128)(2,1)} %get-tuple-element.8.value_ref), custom_call_target="tpu_custom_call" | custom-call | tf_op jit(solution)/shard_map/hand_over/pallas_call | solution.py:675
